TPU v7x, 256 devices: a whole 4x4x8 slice. The times are simulated.
256 devices in a mesh: dp: 4 (over x), fsdp: 16 (over z_hi, y, core), mp: 4 (over z_lo).
Axes of the slice: x: 4, y: 4, z: 8 (z_hi: 2, z_lo: 4; z = z_hi * 4 + z_lo), core: 2. Of those that a mesh axis runs over, the one named last changes fastest.
Arguments:
- tokens_in: bfloat16 [512, 8192], P('dp', 'fsdp'), may hold values from -5 to 5
- weight: bfloat16 [8192, 4, 8192], P('fsdp', 'dp', 'mp'), may hold values from -0.25 to 0.25
- cotangent: bfloat16 [512, 4, 8192], P('dp', None, 'mp'), may hold values from -5 to 5
- row_moment: float32 [8192], P('fsdp'), may hold values from 0.01 to 1
- col_moment: float32 [4, 8192], P('dp', 'mp'), may hold values from 0.01 to 1
Outputs:
- input_grad: bfloat16 [512, 8192], P('dp', ('fsdp', 'mp'))
- row_moment_new: float32 [8192], P('fsdp')
- col_moment_new: float32 [4, 8192], P('dp', 'mp')
- update: float32 [8192, 4, 8192], P('fsdp', 'dp', 'mp')
- update_rms: float32 [], replicated
All inputs are finite; a program needn't handle non-finite values.
Results may differ from a plain program's by a relative error of at most 0.0049.
Values may be sent and summed in bfloat16 or wider, within the bound.
A program may use at most 64 MiB of HBM per device.

v0:
```python
import math

import jax
import jax.numpy as jnp
from jax import lax
from jax.sharding import PartitionSpec as P

D = 8192
HID = 32768
STEP_INDEX = 10


tiny_term = 1e-30
clip_level = 1.0
gelu_coeff = 0.044715


def gelu_slope(values):
    root_term = math.sqrt(2.0 / math.pi)
    tanh_value = jnp.tanh(root_term * (values + gelu_coeff * values * values * values))
    return 0.5 * (1.0 + tanh_value) + 0.5 * values * (1.0 - tanh_value * tanh_value) * root_term * (
        1.0 + 3.0 * gelu_coeff * values * values
    )


def per_device(tokens_in, weight, cotangent, row_moment, col_moment):
    tok_here = tokens_in.shape[0]
    fsdp_count = lax.axis_size("fsdp")
    decay_rate = 1.0 - STEP_INDEX ** (-0.8)
    all_tokens = lax.all_gather(tokens_in, "dp", axis=0, tiled=True)
    full_weight = lax.all_gather(weight, "dp", axis=1, tiled=True)
    share_rows = tok_here // fsdp_count
    hidden_share = lax.psum_scatter(
        jnp.einsum("tr,rkc->tkc", tokens_in, full_weight, preferred_element_type=jnp.float32),
        "fsdp",
        scatter_dimension=0,
        tiled=True,
    )
    offset = lax.axis_index("fsdp") * share_rows
    upstream = lax.dynamic_slice_in_dim(cotangent, offset, share_rows, 0)
    slope_share = (upstream.astype(jnp.float32) * gelu_slope(hidden_share)).astype(jnp.bfloat16)
    slope_group = lax.all_gather(slope_share, "fsdp", axis=0, tiled=True)
    input_terms = jnp.einsum(
        "tkc,rkc->tr", slope_group, full_weight, preferred_element_type=jnp.float32
    )
    slope_mine = lax.all_to_all(slope_group, "dp", split_axis=1, concat_axis=0, tiled=True)
    gradient = jnp.einsum("tr,tkc->rkc", all_tokens, slope_mine, preferred_element_type=jnp.float32)
    input_grad = lax.psum_scatter(input_terms, "mp", scatter_dimension=1, tiled=True).astype(
        jnp.bfloat16
    )
    squares = gradient * gradient + tiny_term
    row_part = jnp.sum(squares, axis=(1, 2))
    col_part = jnp.sum(squares, axis=0)
    row_total = lax.psum(row_part, ("dp", "mp"))
    col_total = lax.psum(col_part, "fsdp")
    row_new = decay_rate * row_moment + (1.0 - decay_rate) * row_total / HID
    col_new = decay_rate * col_moment + (1.0 - decay_rate) * col_total / D
    row_mean = lax.psum(jnp.sum(row_new), "fsdp") / D
    second = row_new[:, None, None] * col_new[None, :, :] / row_mean
    normalized = gradient / jnp.sqrt(second)
    total_squares = lax.psum(jnp.sum(normalized * normalized), ("dp", "fsdp", "mp"))
    update_rms = jnp.sqrt(total_squares / (D * HID))
    update = normalized / jnp.maximum(1.0, update_rms / clip_level)
    return (input_grad, row_new, col_new, update, update_rms)


def solution(mesh):
    in_specs = (
        P("dp", "fsdp"),
        P("fsdp", "dp", "mp"),
        P("dp", None, "mp"),
        P("fsdp"),
        P("dp", "mp"),
    )
    out_specs = (P("dp", ("fsdp", "mp")), P("fsdp"), P("dp", "mp"), P("fsdp", "dp", "mp"), P())
    return jax.shard_map(
        per_device, mesh=mesh, in_specs=in_specs, out_specs=out_specs, check_vma=False
    )
```

profile of v0, /device:TPU:1, one launch (start us, length us, event | category | flops | bytes accessed | tf_op | source)
XLA Modules:
  0.0 511.6 jit_solution(15242849568023071899)
XLA Ops:
  7.2 0.0 copy-start
  7.2 0.0 all-gather.3.cloned.1.call-start
  7.2 0.7 all-gather.3.cloned.1.call-update
  7.9 0.0 reduce-scatter.3.cloned.1.call-start
  8.0 91.4 %all-gather.3.cloned.1.call-done = bf16[512,4,2048]{2,0,1:T(8,128)(2,1)} async-done(((bf16[512,1,2048]{2,0,1:T(8,128)(2,1)}), bf16[512,4,2048]{2,0,1:T(8,128)(2,1)}) %all-gather.3.cloned.1.call-update) | async-done | bytes 8388624 | tf_op jit(solution)/shard_map/all_gather | solution.py:31
  99.3 6.7 %fusion.10 = f32[128,4,2048]{2,0,1:T(8,128)} fusion(bf16[512,4,2048]{2,0,1:T(8,128)(2,1)} %all-gather.3.cloned.1.call-done, bf16[128,512]{1,0:T(8,128)(2,1)} %param.5), kind=kOutput, calls=%fused_computation.17 | convolution fusion | flops 1073741824 | bytes 12713984 | tf_op jit(solution)/shard_map/tr,rkc->tkc/dot_general | solution.py:34
  106.1 0.0 reduce-scatter.3.cloned.1.call-update
  106.1 0.0 all-gather.5.cloned.1.call-start
  106.1 0.1 constant_dynamic-slice_fusion
  106.2 103.9 %reduce-scatter.3.cloned.1.call-done = f32[8,4,2048]{2,0,1:T(8,128)} async-done(((f32[128,4,2048]{2,0,1:T(8,128)}), f32[8,4,2048]{2,0,1:T(8,128)}) %reduce-scatter.3.cloned.1.call-update) | async-done | bytes 262160 | tf_op jit(solution)/shard_map/reduce_scatter | solution.py:33
  210.1 1.8 fusion.9
  211.9 0.0 all-gather.5.cloned.1.call-update
  212.0 62.4 %all-gather.5.cloned.1.call-done = bf16[128,4,2048]{2,0,1:T(8,128)(2,1)} async-done(((bf16[8,4,2048]{2,0,1:T(8,128)(2,1)}), bf16[128,4,2048]{2,0,1:T(8,128)(2,1)}) %all-gather.5.cloned.1.call-update) | async-done | bytes 2097168 | tf_op jit(solution)/shard_map/all_gather | solution.py:42
  274.3 4.5 all-to-all-start
  278.8 0.0 reduce-scatter.5.cloned.1.call-start
  278.9 32.0 %all_gather.11 = bf16[512,512]{1,0:T(8,128)(2,1)S(1)} all-gather(bf16[128,512]{1,0:T(8,128)(2,1)S(1)} %copy-done.1), channel_id=1, replica_groups=mesh['dp'=4,'fsdp'=16,'mp'=4] {'dp'}, dimensions={0}, use_global_device_ids=true | all-gather | bytes 655360 | tf_op jit(solution)/shard_map/all_gather | solution.py:30
  310.9 7.7 %convolution_bitcast_fusion = f32[128,512]{1,0:T(8,128)} fusion(bf16[128,4,2048]{2,0,1:T(8,128)(2,1)} %all-gather.5.cloned.1.call-done, bf16[512,4,2048]{2,0,1:T(8,128)(2,1)} %all-gather.3.cloned.1.call-done), kind=kOutput, calls=%fused_computation.7 | convolution fusion | flops 1073741824 | bytes 10747904 | tf_op jit(solution)/shard_map/tkc,rkc->tr/dot_general | solution.py:43
  318.5 0.0 reduce-scatter.5.cloned.1.call-update
  318.6 0.0 all-to-all-done
  318.6 0.0 copy-start.5
  318.6 0.0 copy-start.4
  318.6 5.0 fusion.1
  323.6 31.6 %psum.28 = f32[512]{0:T(512)S(1)} all-reduce(f32[512]{0:T(512)S(1)} %get-tuple-element.16), channel_id=1, replica_groups=mesh['dp'=4,'fsdp'=16,'mp'=4] {'dp','mp'}, use_global_device_ids=true, to_apply=%region_3.0 | all-reduce | flops 512 | bytes 4096 | tf_op jit(solution)/shard_map/psum | solution.py:54
  355.2 0.6 fusion.12
  355.8 54.0 %all-reduce = (f32[1,2048]{1,0:T(1,128)S(1)}, f32[]{:T(128)}) all-reduce(f32[1,2048]{1,0:T(1,128)S(1)} %bitcast.34, f32[]{:T(128)} %get-tuple-element.19), channel_id=1, replica_groups=mesh['dp'=4,'fsdp'=16,'mp'=4] {'fsdp'}, use_global_device_ids=true, to_apply=%region_5.0 | all-reduce | flops 2049 | bytes 16392 | tf_op jit(solution)/shard_map/psum | solution.py:55
  409.9 0.0 copy-start.2
  410.5 3.8 multiply_reduce_fusion
  414.4 1.5 convert_element_type.11
  415.8 72.6 %psum.31 = f32[]{:T(128)} all-reduce(f32[]{:T(128)} %multiply_reduce_fusion), channel_id=1, replica_groups=mesh['dp'=4,'fsdp'=16,'mp'=4] {'dp','fsdp','mp'}, use_global_device_ids=true, to_apply=%region_9.0 | all-reduce | flops 1 | bytes 8 | tf_op jit(solution)/shard_map/psum | solution.py:61
  489.1 3.9 divide_bitcast_fusion
  493.1 0.0 copy-done.2
  493.1 10.9 %copy.13 = f32[512,1,2048]{2,1,0:T(1,128)} copy(f32[512,1,2048]{0,2,1:T(8,128)} %divide_bitcast_fusion) | data formatting | bytes 8388608
  (9 shorter events, 0.0 us)
Async XLA Ops:
  7.2 99.0 %copy-start = (bf16[128,4,2048]{2,1,0:T(4,128)(2,1)S(1)}, bf16[128,4,2048]{2,1,0:T(4,128)(2,1)}, u32[]{:S(2)}) copy-start(bf16[128,4,2048]{2,1,0:T(4,128)(2,1)} %param.7) | copy-start | bytes 6291460
  7.2 92.1 %all-gather.3.cloned.1.call-start = ((), (), s32[]{:S(2)}) async-start(), calls=%async_computation.3 | async-start | bytes 10485760 | tf_op jit(solution)/shard_map/all_gather | solution.py:31
  7.9 202.2 %reduce-scatter.3.cloned.1.call-start = ((), (), s32[]{:S(2)}) async-start(), calls=%async_computation.4 | async-start | bytes 4456448 | tf_op jit(solution)/shard_map/reduce_scatter | solution.py:33
  106.1 172.8 %copy-start.1 = (bf16[128,512]{1,0:T(8,128)(2,1)S(1)}, bf16[128,512]{1,0:T(8,128)(2,1)}, u32[]{:S(2)}) copy-start(bf16[128,512]{1,0:T(8,128)(2,1)} %param.5) | copy-start | bytes 393220
  106.1 168.3 %all-gather.5.cloned.1.call-start = ((), (), s32[]{:S(2)}) async-start(), calls=%async_computation.5 | async-start | bytes 2228224 | tf_op jit(solution)/shard_map/all_gather | solution.py:42
  274.3 44.2 %all-to-all-start = ((bf16[128,4,2048]{2,0,1:T(8,128)(2,1)}), bf16[128,4,2048]{2,0,1:T(8,128)(2,1)}, u32[]{:S(2)}, u32[]{:S(2)}) async-start(bf16[128,4,2048]{2,0,1:T(8,128)(2,1)} %all-gather.5.cloned.1.call-done), calls=%async_computation.2 | async-start | bytes 4194304 | tf_op jit(solution)/shard_map/all_to_all | solution.py:46
  278.8 135.5 %reduce-scatter.5.cloned.1.call-start = ((), (), s32[]{:S(2)}) async-start(), calls=%async_computation.6 | async-start | bytes 327680 | tf_op jit(solution)/shard_map/reduce_scatter | solution.py:48
  318.6 36.6 %copy-start.5 = (f32[512]{0:T(512)S(1)}, f32[512]{0:T(512)}, u32[]{:S(2)}) copy-start(f32[512]{0:T(512)} %param.8) | copy-start | bytes 6148
  318.6 91.2 %copy-start.4 = (f32[1,2048]{1,0:T(1,128)S(1)}, f32[1,2048]{1,0:T(1,128)}, u32[]{:S(2)}) copy-start(f32[1,2048]{1,0:T(1,128)} %param.9) | copy-start | bytes 24580
  355.8 137.3 %copy-start.3 = (f32[512]{0:T(512)}, f32[512]{0:T(512)S(1)}, u32[]{:S(2)}) copy-start(f32[512]{0:T(512)S(1)} %get-tuple-element.20) | copy-start | bytes 6148
  409.9 83.2 %copy-start.2 = (f32[1,2048]{1,0:T(1,128)}, f32[1,2048]{1,0:T(1,128)S(1)}, u32[]{:S(2)}) copy-start(f32[1,2048]{1,0:T(1,128)S(1)} %multiply_add_fusion.1) | copy-start | bytes 24580
Sparse Core Ops, SparseCore 0:
  9.8 89.4 all-gather.2
  106.2 103.8 reduce-scatter.2
  213.9 60.4 all-gather.4
  318.7 20.1 reduce-scatter.4
where the time goes:
time: 512 us
  waiting for transfers between devices  258 us (50%)
  blocking collectives  190 us (37%)
  matrix products  19.4 us (4%)
  between operations  16.3 us (3%)
  other arithmetic  11.7 us (2%)
  local copies, waits for them, and re-layouts  11 us (2%)
    reduce_scatter x1, waiting for transfers between devices, per_device(): lax.psum_scatter(jnp.einsum('tr,rkc->tkc', tokens_in, full_weight, prefer...  104 us
    all_gather x1, waiting for transfers between devices, per_device(): full_weight = lax.all_gather(weight, 'dp', axis=1, tiled=True)  91.4 us
    psum x1, blocking collectives, per_device(): lax.psum(jnp.sum(normalized * normalized), ('dp', 'fsdp', 'mp'))  72.6 us
    all_gather x1, waiting for transfers between devices, per_device(): slope_group = lax.all_gather(slope_share, 'fsdp', axis=0, tiled=True)  62.4 us
    psum x1, blocking collectives, per_device(): col_total = lax.psum(col_part, 'fsdp')  54 us
    all_gather x1, blocking collectives, per_device(): all_tokens = lax.all_gather(tokens_in, 'dp', axis=0, tiled=True)  32 us
    psum x1, blocking collectives, per_device(): row_total = lax.psum(row_part, ('dp', 'mp'))  31.6 us
    unnamed x13, local copies, waits for them, and re-layouts  10.9 us
  transfers between devices with their start and end apart: 5, of which 3 were waited for; matrix products, arithmetic and copies ran while one was open for 3% of the time, Pallas kernels for 0%

commit v1 on v0

v1 whole, which is shorter than its diff:
```python
import math

import jax
import jax.numpy as jnp
from jax import lax
from jax.sharding import PartitionSpec as P

D = 8192
HID = 32768
STEP_INDEX = 10


tiny_term = 1e-30
clip_level = 1.0
gelu_coeff = 0.044715


def gelu_slope(values):
    root_term = math.sqrt(2.0 / math.pi)
    tanh_value = jnp.tanh(root_term * (values + gelu_coeff * values * values * values))
    return 0.5 * (1.0 + tanh_value) + 0.5 * values * (1.0 - tanh_value * tanh_value) * root_term * (
        1.0 + 3.0 * gelu_coeff * values * values
    )


def per_device(tokens_in, weight, cotangent, row_moment, col_moment):
    tok_here = tokens_in.shape[0]
    fsdp_count = lax.axis_size("fsdp")
    dp_count = lax.axis_size("dp")
    decay_rate = 1.0 - STEP_INDEX ** (-0.8)
    share = tok_here // fsdp_count
    own = weight[:, 0, :]
    tokens = lax.all_gather(tokens_in, "dp", axis=0, tiled=True)
    hidden = jnp.dot(tokens, own, preferred_element_type=jnp.float32)
    hidden = hidden.reshape(dp_count, fsdp_count, share, -1).swapaxes(0, 1).reshape(hidden.shape)
    hidden = lax.psum_scatter(hidden, "fsdp", scatter_dimension=0, tiled=True)
    offset = lax.axis_index("fsdp") * share
    upstream = lax.dynamic_slice_in_dim(cotangent, offset, share, 0).swapaxes(0, 1)
    upstream = lax.all_to_all(upstream, "dp", split_axis=0, concat_axis=0, tiled=True)
    upstream = upstream.reshape(hidden.shape)
    slope = (upstream.astype(jnp.float32) * gelu_slope(hidden)).astype(jnp.bfloat16)
    slope = lax.all_gather(slope, "fsdp", axis=0, tiled=True)
    slope = slope.reshape(fsdp_count, dp_count, share, -1).swapaxes(0, 1).reshape(slope.shape)
    input_terms = jnp.dot(slope, own.T, preferred_element_type=jnp.float32)
    gradient = jnp.dot(tokens.T, slope, preferred_element_type=jnp.float32)
    input_grad = lax.psum_scatter(input_terms, "dp", scatter_dimension=0, tiled=True)
    input_grad = lax.psum_scatter(input_grad, "mp", scatter_dimension=1, tiled=True)
    input_grad = input_grad.astype(jnp.bfloat16)
    squares = gradient * gradient + tiny_term
    row_total = lax.psum(jnp.sum(squares, axis=1), ("dp", "mp"))
    col_total = lax.psum(jnp.sum(squares, axis=0), "fsdp")
    row_new = decay_rate * row_moment + (1.0 - decay_rate) * row_total / HID
    col_new = decay_rate * col_moment + (1.0 - decay_rate) * col_total[None] / D
    shape = gradient * lax.rsqrt(row_new)[:, None] * lax.rsqrt(col_new)
    totals = jnp.stack([jnp.sum(row_new) / 16.0, jnp.sum(shape * shape)])
    totals = lax.psum(totals, ("dp", "fsdp", "mp"))
    row_mean = totals[0] / D
    update_rms = jnp.sqrt(row_mean * totals[1] / (D * HID))
    factor = jnp.sqrt(row_mean) / jnp.maximum(1.0, update_rms / clip_level)
    update = (shape * factor)[:, None, :]
    return (input_grad, row_new, col_new, update, update_rms)


def solution(mesh):
    in_specs = (
        P("dp", "fsdp"),
        P("fsdp", "dp", "mp"),
        P("dp", None, "mp"),
        P("fsdp"),
        P("dp", "mp"),
    )
    out_specs = (P("dp", ("fsdp", "mp")), P("fsdp"), P("dp", "mp"), P("fsdp", "dp", "mp"), P())
    return jax.shard_map(
        per_device, mesh=mesh, in_specs=in_specs, out_specs=out_specs, check_vma=False
    )
```

time: 512 us -> 399 us (0.78)
  waiting for transfers between devices: 258 us -> 165 us
  blocking collectives: 190 us -> 176 us
  matrix products: 19.4 us -> 8.5 us
  local copies, waits for them, and re-layouts: 11 us -> 17.9 us
    all_gather x2 -> x1, waiting for transfers between devices: 154 us -> 62.2 us  [per_device(): slope = lax.all_gather(slope, 'fsdp', axis=0, tiled=True)]
    all_gather x1, blocking collectives: 32 us -> 12.7 us  [per_device(): tokens = lax.all_gather(tokens_in, 'dp', axis=0, tiled=True)]
    dot_general x3, matrix products: 19.4 us -> 8.5 us  [the longest x1 4.97 us: per_device(): gradient = jnp.dot(tokens.T, slope, preferred_element_type=jnp.float32)]
    all_to_all x0 -> x1, blocking collectives: none -> 7.81 us  [per_device(): lax.all_to_all(upstream, 'dp', split_axis=0, concat_axis=0, tiled=True)]
    reduce_scatter x2 -> x3, waiting for transfers between devices: 104 us -> 102 us  [the longest x1 98.8 us: per_device(): hidden = lax.psum_scatter(hidden, 'fsdp', scatter_dimension=0, tiled=True)]
    unnamed x13 -> x12, local copies, waits for them, and re-layouts: 10.9 us -> 12.3 us
  transfers between devices with their start and end apart: 5 -> 4, of which waited for: 3 -> 3; matrix products, arithmetic and copies ran while one was open for 3% -> 7% of each run, Pallas kernels for 0% -> 0%
where the time goes in v1:
time: 399 us; the launch traced here: 398 us
  blocking collectives  176 us (44%)
  waiting for transfers between devices  165 us (41%)
  local copies, waits for them, and re-layouts  17.9 us (4%)
  between operations  17.1 us (4%)
  other arithmetic  13.8 us (3%)
  matrix products  8.5 us (2%)
    reduce_scatter x1, waiting for transfers between devices, per_device(): hidden = lax.psum_scatter(hidden, 'fsdp', scatter_dimension=0, tiled=True)  98.8 us
    psum x1, blocking collectives, per_device(): totals = lax.psum(totals, ('dp', 'fsdp', 'mp'))  72.4 us
    all_gather x1, waiting for transfers between devices, per_device(): slope = lax.all_gather(slope, 'fsdp', axis=0, tiled=True)  62.2 us
    psum x1, blocking collectives, per_device(): col_total = lax.psum(jnp.sum(squares, axis=0), 'fsdp')  49.9 us
    psum x1, blocking collectives, per_device(): row_total = lax.psum(jnp.sum(squares, axis=1), ('dp', 'mp'))  33 us
    all_gather x1, blocking collectives, per_device(): tokens = lax.all_gather(tokens_in, 'dp', axis=0, tiled=True)  12.7 us
    unnamed x12, local copies, waits for them, and re-layouts  12.3 us
  transfers between devices with their start and end apart: 4, of which 3 were waited for; matrix products, arithmetic and copies ran while one was open for 7% of the time, Pallas kernels for 0%

profile of v1, /device:TPU:1, one launch (start us, length us, event | category | flops | bytes accessed | tf_op | source)
XLA Modules:
  0.0 397.9 jit_solution(4721038658305790371)
XLA Ops:
  7.2 0.0 reduce-scatter.4.cloned.1.call-start
  7.2 12.7 %all_gather.6 = bf16[512,512]{1,0:T(8,128)(2,1)S(1)} all-gather(bf16[128,512]{1,0:T(8,128)(2,1)} %param.5), channel_id=1, replica_groups=mesh['dp'=4,'fsdp'=16,'mp'=4] {'dp'}, dimensions={0}, use_global_device_ids=true | all-gather | bytes 655360 | tf_op jit(solution)/shard_map/all_gather | solution.py:33
  19.9 1.2 convolution_bitcast_fusion
  21.2 2.3 copy.12
  23.4 0.0 reduce-scatter.4.cloned.1.call-update
  23.5 0.0 all-gather.2.cloned.1.call-start
  23.5 1.0 constant_dynamic-slice_fusion
  24.5 0.1 copy.18
  24.6 7.8 %all_to_all.5 = bf16[4,8,2048]{2,1,0:T(8,128)(2,1)S(1)} all-to-all(bf16[4,8,2048]{2,1,0:T(8,128)(2,1)S(1)} %bitcast.42), channel_id=1, replica_groups=mesh['dp'=4,'fsdp'=16,'mp'=4] {'dp'}, dimensions={0} | all-to-all | bytes 262144 | tf_op jit(solution)/shard_map/all_to_all | solution.py:39
  32.4 98.8 %reduce-scatter.4.cloned.1.call-done = f32[32,2048]{1,0:T(8,128)} async-done(((f32[512,2048]{1,0:T(8,128)}), f32[32,2048]{1,0:T(8,128)}) %reduce-scatter.4.cloned.1.call-update) | async-done | bytes 262160 | tf_op jit(solution)/shard_map/reduce_scatter | solution.py:36
  131.2 1.8 fusion.11
  133.0 0.0 reduce-scatter.6.cloned.1.call-start
  133.1 62.2 %all-gather.2.cloned.1.call-done = bf16[512,2048]{1,0:T(8,128)(2,1)} async-done(((bf16[32,2048]{1,0:T(8,128)(2,1)}), bf16[512,2048]{1,0:T(8,128)(2,1)}) %all-gather.2.cloned.1.call-update) | async-done | bytes 2097168 | tf_op jit(solution)/shard_map/all_gather | solution.py:42
  195.3 1.7 copy.13
  197.0 1.3 copy-done.1
  198.4 2.3 fusion.3
  200.7 0.0 reduce-scatter.8.cloned.1.call-start
  200.8 5.0 %fusion = (f32[2048]{0:T(1024)S(1)}, f32[512]{0:T(512)S(1)}, f32[2048,512]{1,0:T(8,128)}) fusion(bf16[512,2048]{1,0:T(8,128)(2,1)} %bitcast.39, bf16[512,512]{1,0:T(8,128)(2,1)S(1)} %all_gather.6), kind=kOutput, calls=%fused_computation.4 | convolution fusion | flops 1077933568 | bytes 6825984 | tf_op jit(solution)/shard_map/dot_general | solution.py:45
  205.7 33.0 %psum.21 = f32[512]{0:T(512)S(1)} all-reduce(f32[512]{0:T(512)S(1)} %get-tuple-element.16), channel_id=1, replica_groups=mesh['dp'=4,'fsdp'=16,'mp'=4] {'dp','mp'}, use_global_device_ids=true, to_apply=%region_4.0 | all-reduce | flops 512 | bytes 4096 | tf_op jit(solution)/shard_map/psum | solution.py:50
  238.8 0.6 fusion.12
  240.0 49.9 %psum.22 = f32[2048]{0:T(1024)S(1)} all-reduce(f32[2048]{0:T(1024)S(1)} %get-tuple-element.15), channel_id=1, replica_groups=mesh['dp'=4,'fsdp'=16,'mp'=4] {'fsdp'}, use_global_device_ids=true, to_apply=%region_6.0 | all-reduce | flops 2048 | bytes 16384 | tf_op jit(solution)/shard_map/psum | solution.py:51
  289.9 0.6 fusion.13
  290.5 4.0 %multiply_reduce_fusion = f32[]{:T(128)} fusion(f32[2048,512]{1,0:T(8,128)} %get-tuple-element.23, f32[2048]{0:T(1024)S(1)} %bitcast.43, f32[512]{0:T(512)S(1)} %rsqrt.6), kind=kLoop, calls=%fused_computation.1 | loop fusion | flops 4194303 | bytes 4204548 | tf_op jit(solution)/shard_map/reduce_sum | solution.py:55
  294.6 0.7 pad_maximum_fusion
  295.3 72.4 %psum.23 = f32[2]{0:T(128)S(1)} all-reduce(f32[2]{0:T(128)S(1)} %pad_maximum_fusion), channel_id=1, replica_groups=mesh['dp'=4,'fsdp'=16,'mp'=4] {'dp','fsdp','mp'}, use_global_device_ids=true, to_apply=%region_9.0 | all-reduce | flops 2 | bytes 16 | tf_op jit(solution)/shard_map/psum | solution.py:56
  367.7 0.6 fusion.14
  369.7 0.0 reduce-scatter.6.cloned.1.call-done
  369.8 0.0 reduce-scatter.8.cloned.1.call-update
  369.8 4.6 %multiply_bitcast_fusion = f32[512,1,2048]{0,2,1:T(8,128)} fusion(f32[2048,512]{1,0:T(8,128)} %get-tuple-element.23, f32[]{:T(128)S(6)} %div.35, f32[2048]{0:T(1024)S(1)} %bitcast.44, f32[512]{0:T(512)S(1)} %rsqrt.6), kind=kLoop, calls=%fused_computation | loop fusion | flops 3145728 | bytes 8398852 | tf_op jit(solution)/shard_map/broadcast_in_dim | solution.py:60
  374.4 10.9 %copy.14 = f32[512,1,2048]{2,1,0:T(1,128)} copy(f32[512,1,2048]{0,2,1:T(8,128)} %multiply_bitcast_fusion) | data formatting | bytes 8388608
  385.3 3.5 reduce-scatter.8.cloned.1.call-done
  388.8 1.5 convert_element_type.15
  (13 shorter events, 0.1 us)
Async XLA Ops:
  7.2 12.7 %copy-start = (bf16[512,1,2048]{2,0,1:T(8,128)(2,1)S(1)}, bf16[512,1,2048]{2,0,1:T(8,128)(2,1)}, u32[]{:S(2)}) copy-start(bf16[512,1,2048]{2,0,1:T(8,128)(2,1)} %param.6) | copy-start | bytes 6291460
  7.2 124.0 %reduce-scatter.4.cloned.1.call-start = ((), (), s32[]{:S(2)}) async-start(), calls=%async_computation.4 | async-start | bytes 4456448 | tf_op jit(solution)/shard_map/reduce_scatter | solution.py:36
  23.5 171.8 %all-gather.2.cloned.1.call-start = ((), (), s32[]{:S(2)}) async-start(), calls=%async_computation.5 | async-start | bytes 2228224 | tf_op jit(solution)/shard_map/all_gather | solution.py:42
  133.0 236.7 %reduce-scatter.6.cloned.1.call-start = ((), (), s32[]{:S(2)}) async-start(), calls=%async_computation.6 | async-start | bytes 1310720 | tf_op jit(solution)/shard_map/reduce_scatter | solution.py:46
  197.0 1.4 copy-start.1
  200.7 38.1 %copy-start.4 = (f32[512]{0:T(512)S(1)}, f32[512]{0:T(512)}, u32[]{:S(2)}) copy-start(f32[512]{0:T(512)} %param.8) | copy-start | bytes 6148
  200.7 89.2 %copy-start.3 = (f32[1,2048]{1,0:T(1,128)S(1)}, f32[1,2048]{1,0:T(1,128)}, u32[]{:S(2)}) copy-start(f32[1,2048]{1,0:T(1,128)} %param.9) | copy-start | bytes 24580
  200.7 188.1 %reduce-scatter.8.cloned.1.call-start = ((), (), s32[]{:S(2)}) async-start(), calls=%async_computation.7 | async-start | bytes 327680 | tf_op jit(solution)/shard_map/reduce_scatter | solution.py:47
  239.4 135.1 %copy-start.2 = (f32[512]{0:T(512)}, f32[512]{0:T(512)S(1)}, u32[]{:S(2)}) copy-start(f32[512]{0:T(512)S(1)} %get-tuple-element.18) | copy-start | bytes 6148
Sparse Core Ops, SparseCore 0:
  23.6 107.5 reduce-scatter.3
  134.9 60.3 all-gather.1
  200.8 19.7 reduce-scatter.5
  369.9 18.8 reduce-scatter.7

commit v2 on v0

v2 whole, which is shorter than its diff:
```python
import math

import jax
import jax.numpy as jnp
from jax import lax
from jax.experimental import pallas as pl
from jax.experimental.pallas import tpu as pltpu
from jax.sharding import PartitionSpec as P

MESH = pl.DeviceIdType.MESH
D = 8192
HID = 32768
STEP_INDEX = 10
DECAY = 1.0 - STEP_INDEX ** (-0.8)

tiny_term = 1e-30
clip_level = 1.0
gelu_coeff = 0.044715

F32 = jnp.float32
BF16 = jnp.bfloat16

CHUNK = 128
HALF = 64
COLS = 256
ROWS = 512
GROUPS = 8
ORDER = (0, 1, 3, 2)
UP = (0, 1)


def gelu_slope(values):
    root_term = math.sqrt(2.0 / math.pi)
    tanh_value = jnp.tanh(root_term * (values + gelu_coeff * values * values * values))
    return 0.5 * (1.0 + tanh_value) + 0.5 * values * (1.0 - tanh_value * tanh_value) * root_term * (
        1.0 + 3.0 * gelu_coeff * values * values
    )


class Slots:
    def __init__(self):
        self.numbers = {}

    def __call__(self, *key):
        return self.numbers.setdefault(key, len(self.numbers))


N_SEMS = 112


def main_kernel(
    tok, wgt, cot, row_mom, col_mom,
    grad_out, inp_out, row_out, rcol_out, col_out, scal_out,
    t_own, t_peer, t_tr, w_own, w_peer, ct,
    sd, rd, sn, rm, rp, hn, ho, zs, zr, sl, grad, terms,
    i_out, i_in, i_sum, j_out, j_in,
    row_acc, row_buf, col_buf, one_buf, two_buf,
    send, recv, local, peer_send, peer_recv,
):
    d, f, m = lax.axis_index("dp"), lax.axis_index("fsdp"), lax.axis_index("mp")
    c, y, zh = f % 2, (f // 2) % 4, f // 8
    fid = lambda zz, yy, cc: (zz * 4 + yy) * 2 + cc
    core_dev = {"fsdp": fid(zh, y, 1 - c)}
    up_dev = {"fsdp": fid(zh, (y + 1) % 4, c)}
    down_dev = {"fsdp": fid(zh, (y + 3) % 4, c)}
    z_dev = {"fsdp": fid(1 - zh, y, c)}
    number = Slots()
    sent = []

    def start(src, dst, key, dev):
        i = number(*key)
        copy = pltpu.make_async_remote_copy(
            src_ref=src, dst_ref=dst, send_sem=send.at[i], recv_sem=recv.at[i],
            device_id=dev, device_id_type=MESH,
        )
        copy.start()
        sent.append(copy)

    def wait(dst, key):
        i = number(*key)
        pltpu.make_async_remote_copy(
            src_ref=dst, dst_ref=dst, send_sem=send.at[i], recv_sem=recv.at[i],
            device_id=core_dev, device_id_type=MESH,
        ).wait_recv()

    def x_dev(r):
        return {"dp": (d + r) % 4}

    w_loads = {}
    for rel in (2, 3, 1, 0):
        for cc in (0, 1):
            g = (c if cc == 0 else 1 - c) * 4 + (y + rel) % 4
            copy = pltpu.make_async_copy(
                wgt.at[:, pl.ds(pl.multiple_of(g * COLS, COLS), COLS)], w_own.at[g],
                local.at[rel * 2 + cc],
            )
            copy.start()
            w_loads[rel, cc] = copy
    t_load = pltpu.make_async_copy(tok, t_own.at[d], local.at[8])
    t_load.start()
    c_load = pltpu.make_async_copy(cot.at[d], ct.at[d], local.at[9])
    c_load.start()

    barrier = pltpu.get_barrier_semaphore()

    def greet(j, carry):
        pl.semaphore_signal(barrier, inc=1, device_id={"fsdp": (f + j) % 16}, device_id_type=MESH)
        pl.semaphore_signal(
            barrier, inc=1, device_id={"dp": (d + j // 4) % 4, "mp": (m + j % 4) % 4},
            device_id_type=MESH,
        )
        return carry

    lax.fori_loop(1, 16, greet, 0)
    pl.semaphore_wait(barrier, 30)

    for r in (1, 3, 2):
        start(tok, t_own.at[d], ("tok", r), x_dev(r))
    start(tok, t_peer.at[d], ("tpeer", 0), core_dev)
    for rel in (2, 3, 1, 0):
        yy = (y + rel) % 4
        g = (1 - c) * 4 + yy
        start(
            wgt.at[:, pl.ds(pl.multiple_of(g * COLS, COLS), COLS)], w_peer.at[yy],
            ("w", rel), core_dev,
        )
    for r in (1, 3, 2):
        start(cot.at[(d + r) % 4], ct.at[d], ("ct", r), x_dev(r))

    have_w = set()

    def product(k, rel):
        dk, yy = (d + k) % 4, (y + rel) % 4
        if rel not in have_w:
            have_w.add(rel)
            w_loads[rel, 0].wait()
            wait(w_peer.at[yy], ("w", rel))
        return jnp.dot(
            t_own[dk], w_own[c * 4 + yy], preferred_element_type=F32
        ) + jnp.dot(t_peer[dk], w_peer[yy], preferred_element_type=F32)

    def stage_tokens(k):
        dk = (d + k) % 4
        if k == 0:
            t_load.wait()
        else:
            wait(t_own.at[dk], ("tok", 4 - k))
            start(t_own.at[dk], t_peer.at[dk], ("tpeer", k), core_dev)

    def stage_products(k):
        dk = (d + k) % 4
        wait(t_peer.at[dk], ("tpeer", k))
        sd[k] = product(k, 2).astype(BF16)
        start(sd.at[k], rd.at[k], ("rd", k), up_dev if k in UP else down_dev)
        if k in UP:
            sn[k, 0] = product(k, 3).astype(BF16)
            start(sn.at[k, 0], rp.at[k], ("rp", k), down_dev)
            hn[k] = product(k, 1)
        else:
            sn[k, 0] = product(k, 1).astype(BF16)
            start(sn.at[k, 0], rm.at[k], ("rm", k), up_dev)
            hn[k] = product(k, 3)
        ho[k] = product(k, 0)

    def stage_diagonal(k):
        wait(rd.at[k], ("rd", k))
        sn[k, 1] = (hn[k] + rd[k].astype(F32)).astype(BF16)
        if k in UP:
            start(sn.at[k, 1], rm.at[k], ("rm", k), up_dev)
        else:
            start(sn.at[k, 1], rp.at[k], ("rp", k), down_dev)

    mine = pl.ds(pl.multiple_of(zh * HALF, HALF), HALF)
    other = pl.ds(pl.multiple_of((1 - zh) * HALF, HALF), HALF)

    def stage_sum(k):
        wait(rm.at[k], ("rm", k))
        wait(rp.at[k], ("rp", k))
        ho[k] = ho[k] + rm[k].astype(F32) + rp[k].astype(F32)
        zs[k] = ho[k, other].astype(BF16)
        start(zs.at[k], zr.at[k], ("z", k), z_dev)

    g_own = c * 4 + y

    def rows_of(k, zz):
        dk = (d + k) % 4
        return pl.ds(pl.multiple_of(dk * CHUNK + zz * HALF, HALF), HALF)

    def chunk_of(k):
        dk = (d + k) % 4
        return pl.ds(pl.multiple_of(dk * CHUNK, CHUNK), CHUNK)

    def stage_slope(k):
        dk = (d + k) % 4
        wait(zr.at[k], ("z", k))
        if k == 0:
            c_load.wait()
        else:
            wait(ct.at[dk], ("ct", 4 - k))
        hidden = ho[k, mine] + zr[k].astype(F32)
        sl[g_own, rows_of(k, zh)] = (ct[dk].astype(F32) * gelu_slope(hidden)).astype(BF16)
        block = sl.at[g_own, rows_of(k, zh)]
        start(block, block, ("zs", k), z_dev)

    def stage_spread(k):
        wait(sl.at[g_own, rows_of(k, 1 - zh)], ("zs", k))
        block = sl.at[g_own, chunk_of(k)]
        start(block, block, ("am", k), up_dev)
        start(block, block, ("ap", k), down_dev)
        start(block, block, ("core", 0, k), core_dev)

    def stage_down(k):
        block = sl.at[c * 4 + (y + 3) % 4, chunk_of(k)]
        wait(block, ("am", k))
        if k in UP:
            start(block, block, ("ad", k), up_dev)
        start(block, block, ("core", 3, k), core_dev)

    def stage_up(k):
        block = sl.at[c * 4 + (y + 1) % 4, chunk_of(k)]
        wait(block, ("ap", k))
        if k not in UP:
            start(block, block, ("ad", k), down_dev)
        start(block, block, ("core", 1, k), core_dev)

    def stage_far(k):
        block = sl.at[c * 4 + (y + 2) % 4, chunk_of(k)]
        wait(block, ("ad", k))
        start(block, block, ("core", 2, k), core_dev)

    first = []

    def group(rel, cc):
        g = (c if cc == 0 else 1 - c) * 4 + (y + rel) % 4
        if cc == 1:
            w_loads[rel, 1].wait()
            for k in ORDER:
                wait(sl.at[g, chunk_of(k)], ("core", rel, k))
        value = jnp.dot(t_tr[...], sl[g], preferred_element_type=F32)
        grad[g] = value
        copy = pltpu.make_async_copy(grad.at[g], grad_out.at[g], local.at[10 + rel * 2 + cc])
        copy.start()
        squares = value * value + tiny_term
        col_buf[f, g] = jnp.sum(squares, axis=0, keepdims=True)
        lanes = squares[:, :128] + squares[:, 128:]
        part = lax.dot_general(
            sl[g], w_own[g], (((1,), (1,)), ((), ())), preferred_element_type=F32
        )
        if first:
            row_acc[...] += lanes
            terms[...] += part
        else:
            row_acc[...] = lanes
            terms[...] = part
        first.append(copy)

    stages = (stage_products, stage_diagonal, stage_sum, stage_slope, stage_spread)
    stage_tokens(0)
    for step in range(4 + len(stages) - 1):
        if step == 0:
            stage_products(ORDER[0])
            stage_tokens(1)
            stage_tokens(3)
            continue
        if step == 2:
            stage_tokens(2)
        for s, stage in enumerate(stages):
            if 0 <= step - s < 4:
                stage(ORDER[step - s])
        if step == 3:
            for k in ORDER:
                dk = (d + k) % 4
                t_tr[:, pl.ds(pl.multiple_of(dk * CHUNK, CHUNK), CHUNK)] = t_own[dk].T
    for k in ORDER:
        stage_down(k)
        stage_up(k)
        if k == 1:
            group(0, 0)
    group(0, 1)
    group(3, 0)
    stage_far(0)
    stage_far(1)
    group(1, 0)
    stage_far(3)
    stage_far(2)
    group(3, 1)
    group(1, 1)
    group(2, 0)
    group(2, 1)

    me = d * 4 + m
    row_buf[me] = jnp.sum(row_acc[...].T, axis=0, keepdims=True)

    def to_fsdp(buf, slot, base):
        def one(j, carry):
            pltpu.make_async_remote_copy(
                src_ref=buf.at[slot], dst_ref=buf.at[slot], send_sem=peer_send.at[base + j],
                recv_sem=peer_recv.at[base + j], device_id={"fsdp": (f + j) % 16},
                device_id_type=MESH,
            ).start()
            return carry

        lax.fori_loop(1, 16, one, 0)

    def from_fsdp(buf, base):
        def one(j, carry):
            came = (f + 16 - j) % 16
            pltpu.make_async_remote_copy(
                src_ref=buf.at[came], dst_ref=buf.at[came], send_sem=peer_send.at[base + j],
                recv_sem=peer_recv.at[base + j], device_id={"fsdp": (f + j) % 16},
                device_id_type=MESH,
            ).wait()
            return carry

        lax.fori_loop(1, 16, one, 0)

    def to_plane(buf, slot, base):
        def one(j, carry):
            pltpu.make_async_remote_copy(
                src_ref=buf.at[slot], dst_ref=buf.at[slot], send_sem=peer_send.at[base + j],
                recv_sem=peer_recv.at[base + j],
                device_id={"dp": (d + j // 4) % 4, "mp": (m + j % 4) % 4},
                device_id_type=MESH,
            ).start()
            return carry

        lax.fori_loop(1, 16, one, 0)

    def from_plane(buf, base):
        def one(j, carry):
            came = ((d + 4 - j // 4) % 4) * 4 + (m + 4 - j % 4) % 4
            pltpu.make_async_remote_copy(
                src_ref=buf.at[came], dst_ref=buf.at[came], send_sem=peer_send.at[base + j],
                recv_sem=peer_recv.at[base + j],
                device_id={"dp": (d + j // 4) % 4, "mp": (m + j % 4) % 4},
                device_id_type=MESH,
            ).wait()
            return carry

        lax.fori_loop(1, 16, one, 0)

    to_plane(row_buf, me, 0)
    to_fsdp(col_buf, f, 16)

    for r in (2, 1, 3):
        dr = (d + r) % 4
        i_out[r] = terms[pl.ds(pl.multiple_of(dr * CHUNK, CHUNK), CHUNK)].astype(BF16)
        start(i_out.at[r], i_in.at[r], ("ix", r), x_dev(r))

    from_plane(row_buf, 0)
    total = row_buf[0]
    for j in range(1, 16):
        total = total + row_buf[j]
    row_new = DECAY * row_mom[...] + (1.0 - DECAY) * total / HID
    row_out[...] = row_new
    rcol = jnp.broadcast_to(lax.rsqrt(row_new), (128, ROWS)).T
    rcol_out[...] = rcol
    row_acc[...] = rcol * rcol
    from_fsdp(col_buf, 16)
    total = col_buf[0]
    for j in range(1, 16):
        total = total + col_buf[j]
    col_new = DECAY * col_mom[...] + (1.0 - DECAY) * total / D
    col_out[...] = col_new

    def weigh(b, carry):
        rows = pl.ds(pl.multiple_of(b * 64, 64), 64)
        acc = jnp.zeros((64, 128), F32)
        for g in range(GROUPS):
            inverse = 1.0 / col_out[g]
            piece = grad[g, rows]
            piece = piece * piece * inverse
            acc = acc + piece[:, :128] + piece[:, 128:]
        return carry + jnp.sum(acc * row_acc[rows], axis=0, keepdims=True)

    u_lanes = lax.fori_loop(0, 8, weigh, jnp.zeros((1, 128), F32))
    a_lanes = (row_new[:, :128] + row_new[:, 128:256]) + (row_new[:, 256:384] + row_new[:, 384:])
    one_buf[f, :, :128] = u_lanes
    one_buf[f, :, 128:] = a_lanes
    to_fsdp(one_buf, f, 32)
    from_fsdp(one_buf, 32)
    total = one_buf[0]
    for j in range(1, 16):
        total = total + one_buf[j]
    two_buf[me] = total
    to_plane(two_buf, me, 48)

    acc = terms[pl.ds(pl.multiple_of(d * CHUNK, CHUNK), CHUNK)]
    for r in (1, 3, 2):
        wait(i_in.at[r], ("ix", r))
        acc = acc + i_in[r].astype(F32)
    i_sum[...] = acc
    for r in (1, 3, 2):
        mr = (m + r) % 4
        j_out[r] = i_sum[:, pl.ds(pl.multiple_of(mr * 128, 128), 128)].astype(BF16)
        start(j_out.at[r], j_in.at[r], ("jz", r), {"mp": mr})

    from_plane(two_buf, 48)
    total = two_buf[0]
    for j in range(1, 16):
        total = total + two_buf[j]
    scal_out[:, :128] = total[:, :128]
    scal_out[:, 128:] = two_buf[me][:, 128:]

    acc = i_sum[:, pl.ds(pl.multiple_of(m * 128, 128), 128)]
    for r in (1, 3, 2):
        wait(j_in.at[r], ("jz", r))
        acc = acc + j_in[r].astype(F32)
    inp_out[...] = acc.astype(BF16)

    for copy in sent:
        copy.wait_send()
    for copy in first:
        copy.wait()
    assert len(number.numbers) <= N_SEMS, len(number.numbers)


def last_kernel(grad, rcol, row_new, col_new, scal, inp, upd_out, row_out, col_out, inp_out, rms_out):
    total = jnp.sum(scal[:, :128], axis=1, keepdims=True)
    mean = jnp.sum(scal[:, 128:], axis=1, keepdims=True) / D
    rms = jnp.sqrt(mean * total / (D * HID))
    factor = jnp.sqrt(mean) / jnp.maximum(1.0, rms / clip_level)
    rows = grad.shape[1]
    left = rcol[...] * factor
    for g in range(GROUPS):
        right = lax.rsqrt(col_new[g])
        for h in (0, 1):
            lanes = slice(h * 128, h * 128 + 128)
            upd_out[pl.ds(2 * g + h, rows, stride=16), :] = grad[g, :, lanes] * left * right[:, lanes]

    @pl.when(pl.program_id(0) == 0)
    def _():
        row_out[...] = row_new[...]
        col_out[...] = col_new[...]
        inp_out[...] = inp[...]
        rms_out[...] = rms


def per_device(tokens_in, weight, cotangent, row_moment, col_moment):
    f = lax.axis_index("fsdp")
    c, y, zh = f % 2, (f // 2) % 4, f // 8
    upstream = lax.dynamic_slice(cotangent, (zh * HALF, 0, (c * 4 + y) * COLS), (HALF, 4, COLS))
    upstream = upstream.swapaxes(0, 1)
    vmem = pl.BlockSpec(memory_space=pltpu.VMEM)
    hbm = pl.BlockSpec(memory_space=pl.ANY)
    sds = jax.ShapeDtypeStruct
    grad, inp, row_new, rcol, col_new, scal = pl.pallas_call(
        main_kernel,
        name="main",
        out_shape=(
            sds((GROUPS, ROWS, COLS), F32),
            sds((CHUNK, 128), BF16),
            sds((1, ROWS), F32),
            sds((ROWS, 128), F32),
            sds((GROUPS, 1, COLS), F32),
            sds((1, 256), F32),
        ),
        in_specs=[hbm, hbm, hbm, vmem, vmem],
        out_specs=(hbm, vmem, vmem, vmem, vmem, vmem),
        scratch_shapes=[
            pltpu.VMEM((4, CHUNK, ROWS), BF16),
            pltpu.VMEM((4, CHUNK, ROWS), BF16),
            pltpu.VMEM((ROWS, 4 * CHUNK), BF16),
            pltpu.VMEM((GROUPS, ROWS, COLS), BF16),
            pltpu.VMEM((4, ROWS, COLS), BF16),
            pltpu.VMEM((4, HALF, COLS), BF16),
            pltpu.VMEM((4, CHUNK, COLS), BF16),
            pltpu.VMEM((4, CHUNK, COLS), BF16),
            pltpu.VMEM((4, 2, CHUNK, COLS), BF16),
            pltpu.VMEM((4, CHUNK, COLS), BF16),
            pltpu.VMEM((4, CHUNK, COLS), BF16),
            pltpu.VMEM((4, CHUNK, COLS), F32),
            pltpu.VMEM((4, CHUNK, COLS), F32),
            pltpu.VMEM((4, HALF, COLS), BF16),
            pltpu.VMEM((4, HALF, COLS), BF16),
            pltpu.VMEM((GROUPS, 4 * CHUNK, COLS), BF16),
            pltpu.VMEM((GROUPS, ROWS, COLS), F32),
            pltpu.VMEM((4 * CHUNK, ROWS), F32),
            pltpu.VMEM((4, CHUNK, ROWS), BF16),
            pltpu.VMEM((4, CHUNK, ROWS), BF16),
            pltpu.VMEM((CHUNK, ROWS), F32),
            pltpu.VMEM((4, CHUNK, 128), BF16),
            pltpu.VMEM((4, CHUNK, 128), BF16),
            pltpu.VMEM((ROWS, 128), F32),
            pltpu.VMEM((16, 1, ROWS), F32),
            pltpu.VMEM((16, GROUPS, 1, COLS), F32),
            pltpu.VMEM((16, 1, 256), F32),
            pltpu.VMEM((16, 1, 256), F32),
            pltpu.SemaphoreType.DMA((N_SEMS,)),
            pltpu.SemaphoreType.DMA((N_SEMS,)),
            pltpu.SemaphoreType.DMA((18,)),
            pltpu.SemaphoreType.DMA((64,)),
            pltpu.SemaphoreType.DMA((64,)),
        ],
        compiler_params=pltpu.CompilerParams(
            collective_id=0, has_side_effects=True, vmem_limit_bytes=44 * 1024 * 1024
        ),
        cost_estimate=pl.CostEstimate(flops=3 * 2**30, bytes_accessed=8 * 2**20, transcendentals=2**16),
    )(
        tokens_in,
        weight.reshape(ROWS, GROUPS * COLS),
        upstream,
        row_moment.reshape(1, ROWS),
        col_moment.reshape(GROUPS, 1, COLS),
    )
    steps = 4
    rows = ROWS // steps
    whole = lambda *shape: pl.BlockSpec(shape, lambda i: (0,) * len(shape))
    update, row_new, col_new, input_grad, rms = pl.pallas_call(
        last_kernel,
        name="last",
        grid=(steps,),
        out_shape=(
            sds((ROWS * 16, 128), F32),
            sds((1, ROWS), F32),
            sds((GROUPS, 1, COLS), F32),
            sds((CHUNK, 128), BF16),
            sds((1, 1), F32),
        ),
        in_specs=[
            pl.BlockSpec((GROUPS, rows, COLS), lambda i: (0, i, 0)),
            pl.BlockSpec((rows, 128), lambda i: (i, 0)),
            whole(1, ROWS),
            whole(GROUPS, 1, COLS),
            whole(1, 256),
            whole(CHUNK, 128),
        ],
        out_specs=(
            pl.BlockSpec((rows * 16, 128), lambda i: (i, 0)),
            whole(1, ROWS),
            whole(GROUPS, 1, COLS),
            whole(CHUNK, 128),
            whole(1, 1),
        ),
        compiler_params=pltpu.CompilerParams(vmem_limit_bytes=44 * 1024 * 1024),
    )(grad, rcol, row_new, col_new, scal, inp)
    return (
        input_grad,
        row_new.reshape(ROWS),
        col_new.reshape(1, GROUPS * COLS),
        update.reshape(ROWS, 1, GROUPS * COLS),
        rms.reshape(()),
    )


def solution(mesh):
    in_specs = (
        P("dp", "fsdp"),
        P("fsdp", "dp", "mp"),
        P("dp", None, "mp"),
        P("fsdp"),
        P("dp", "mp"),
    )
    out_specs = (P("dp", ("fsdp", "mp")), P("fsdp"), P("dp", "mp"), P("fsdp", "dp", "mp"), P())
    return jax.shard_map(
        per_device, mesh=mesh, in_specs=in_specs, out_specs=out_specs, check_vma=False
    )
```

time: 512 us -> 88.6 us (0.17)
  waiting for transfers between devices: 258 us -> 0 us
  blocking collectives: 190 us -> 0 us
  Pallas kernels: 0 us -> 82.2 us
  matrix products: 19.4 us -> 0 us
  between operations: 16.3 us -> 0.72 us
  other arithmetic: 11.7 us -> 0 us
  local copies, waits for them, and re-layouts: 11 us -> 5.48 us
    psum x3 -> x0, blocking collectives: 158 us -> none  [the longest x1 72.6 us: per_device(): lax.psum(jnp.sum(normalized * normalized), ('dp', 'fsdp', 'mp'))]
    all_gather x2 -> x0, waiting for transfers between devices: 154 us -> none  [the longest x1 91.4 us: per_device(): full_weight = lax.all_gather(weight, 'dp', axis=1, tiled=True)]
    reduce_scatter x2 -> x0, waiting for transfers between devices: 104 us -> none  [the longest x1 104 us: per_device(): lax.psum_scatter(jnp.einsum('tr,rkc->tkc', tokens_in, full_weight, prefer...]
    pallas_call x0 -> x2, Pallas kernels: none -> 82.2 us  [the longest x1 78 us: per_device(): pl.pallas_call(main_kernel, name='main', out_shape=(sds((GROUPS, ROWS, CO...]
    all_gather x1 -> x0, blocking collectives: 32 us -> none  [per_device(): all_tokens = lax.all_gather(tokens_in, 'dp', axis=0, tiled=True)]
    dot_general x3 -> x0, matrix products: 19.4 us -> none  [the longest x1 7.65 us: per_device(): jnp.einsum('tkc,rkc->tr', slope_group, full_weight, preferred_element_typ...]
    unnamed x13 -> x11, local copies, waits for them, and re-layouts: 10.9 us -> 5.42 us
  transfers between devices with their start and end apart: 5 -> 0, of which waited for: 3 -> 0; matrix products, arithmetic and copies ran while one was open for 3% -> 0% of each run, Pallas kernels for 0% -> 0%
where the time goes in v2:
time: 88.6 us; the launch traced here: 88.4 us
  Pallas kernels  82.2 us (93%)
  local copies, waits for them, and re-layouts  5.48 us (6%)
    pallas_call x1, Pallas kernels, per_device(): pl.pallas_call(main_kernel, name='main', out_shape=(sds((GROUPS, ROWS, CO...  78 us
    unnamed x11, local copies, waits for them, and re-layouts  5.42 us
    pallas_call x1, Pallas kernels, per_device(): pl.pallas_call(last_kernel, name='last', grid=(steps,), out_shape=(sds((R...  4.15 us

profile of v2, /device:TPU:1, one launch (start us, length us, event | category | flops | bytes accessed | tf_op | source)
XLA Modules:
  0.0 88.4 jit_solution(13148291887343866460)
XLA Ops:
  0.6 0.0 copy-start
  0.7 1.5 %copy-done = bf16[128,4,2048]{2,1,0:T(4,128)(2,1)S(1)} copy-done((bf16[128,4,2048]{2,1,0:T(4,128)(2,1)S(1)}, bf16[128,4,2048]{2,1,0:T(4,128)(2,1)}, u32[]{:S(2)}) %copy-start) | copy-done | bytes 2097176
  2.2 0.1 constant_dynamic-slice_fusion
  2.3 0.0 copy-start.1
  2.3 1.6 %copy-done.1 = bf16[512,1,2048]{2,0,1:T(8,128)(2,1)S(1)} copy-done((bf16[512,1,2048]{2,0,1:T(8,128)(2,1)S(1)}, bf16[512,1,2048]{2,0,1:T(8,128)(2,1)}, u32[]{:S(2)}) %copy-start.1) | copy-done | bytes 2097176
  3.9 0.0 copy-start.2
  3.9 0.9 %copy-done.2 = bf16[128,512]{1,0:T(8,128)(2,1)S(1)} copy-done((bf16[128,512]{1,0:T(8,128)(2,1)S(1)}, bf16[128,512]{1,0:T(8,128)(2,1)}, u32[]{:S(2)}) %copy-start.2) | copy-done | bytes 131096
  4.8 0.0 copy-start.3
  4.8 0.7 copy-done.3
  5.5 0.0 copy-start.4
  5.5 0.7 copy-done.4
  6.2 78.0 %main.1 = (f32[8,512,256]{2,1,0:T(8,128)S(1)}, bf16[128,128]{1,0:T(8,128)(2,1)S(1)}, f32[1,512]{1,0:T(1,128)S(1)}, f32[512,128]{1,0:T(8,128)S(1)}, f32[8,1,256]{2,1,0:T(1,128)S(1)}, /*index=5*/f32[1,256]{1,0:T(1,128)S(1)}) custom-call(bf16[128,512]{1,0:T(8,128)(2,1)S(1)} %copy-done.2, bf16[512,2048]{1,0:T(8,128)(2,1)S(1)} %bitcast.11, ...), custom_call_target="tpu_custom_call" | custom-call | flops 3221225472 | bytes 8388608 | tf_op jit(solution)/shard_map/main/pallas_call | solution.py:447
  84.2 4.2 %last.1 = (f32[8192,128]{1,0:T(8,128)}, f32[1,512]{1,0:T(1,128)}, f32[8,1,256]{2,1,0:T(1,128)}, bf16[128,128]{1,0:T(8,128)(2,1)}, f32[1,1]{1,0:T(1,128)}) custom-call(f32[8,512,256]{2,1,0:T(8,128)S(1)} %get-tuple-element.16.grad, f32[512,128]{1,0:T(8,128)S(1)} %get-tuple-element.17.rcol, f32[1,512]{1,0:T(1,128)S(1)} %get-tuple-element.18.row_new, ...), custom_call_target="tpu_custom_call" | custom-call | tf_op jit(solution)/shard_map/last/pallas_call | solution.py:509
  (1 shorter events, 0.0 us)
Async XLA Ops:
  0.6 1.6 %copy-start = (bf16[128,4,2048]{2,1,0:T(4,128)(2,1)S(1)}, bf16[128,4,2048]{2,1,0:T(4,128)(2,1)}, u32[]{:S(2)}) copy-start(bf16[128,4,2048]{2,1,0:T(4,128)(2,1)} %param.7) | copy-start | bytes 6291460
  2.3 1.6 %copy-start.1 = (bf16[512,1,2048]{2,0,1:T(8,128)(2,1)S(1)}, bf16[512,1,2048]{2,0,1:T(8,128)(2,1)}, u32[]{:S(2)}) copy-start(bf16[512,1,2048]{2,0,1:T(8,128)(2,1)} %param.6) | copy-start | bytes 6291460
  3.9 0.9 %copy-start.2 = (bf16[128,512]{1,0:T(8,128)(2,1)S(1)}, bf16[128,512]{1,0:T(8,128)(2,1)}, u32[]{:S(2)}) copy-start(bf16[128,512]{1,0:T(8,128)(2,1)} %tok.1) | copy-start | bytes 393220
  4.8 0.7 copy-start.3
  5.5 0.7 copy-start.4

commit v3 on v2

--- a/solution.py
+++ b/solution.py
@@ -21,12 +21,12 @@
 BF16 = jnp.bfloat16
 
 CHUNK = 128
-HALF = 64
 COLS = 256
 ROWS = 512
 GROUPS = 8
 ORDER = (0, 1, 3, 2)
-UP = (0, 1)
+FIRST = ((0, 0), (0, 1), (3, 0), (1, 0), (3, 1), (1, 1))
+LAST = ((2, 0), (2, 1))
 
 
 def gelu_slope(values):
@@ -50,20 +50,19 @@
 
 def main_kernel(
     tok, wgt, cot, row_mom, col_mom,
-    grad_out, inp_out, row_out, rcol_out, col_out, scal_out,
-    t_own, t_peer, t_tr, w_own, w_peer, ct,
-    sd, rd, sn, rm, rp, hn, ho, zs, zr, sl, grad, terms,
-    i_out, i_in, i_sum, j_out, j_in,
-    row_acc, row_buf, col_buf, one_buf, two_buf,
+    grad, inp_out, row_out, rcol_out, col_out, scal_out,
+    t_own, t_peer, t_tr, w_own, w_peer, c_raw, c_out, ct,
+    so, rr, ho, zs, zr, sl, terms,
+    i_out, i_in, i_sum, j_out, j_in, r_mom, c_mom,
+    row_acc, row_buf, col_a, col_b, one_buf, two_buf,
     send, recv, local, peer_send, peer_recv,
 ):
     d, f, m = lax.axis_index("dp"), lax.axis_index("fsdp"), lax.axis_index("mp")
     c, y, zh = f % 2, (f // 2) % 4, f // 8
     fid = lambda zz, yy, cc: (zz * 4 + yy) * 2 + cc
     core_dev = {"fsdp": fid(zh, y, 1 - c)}
-    up_dev = {"fsdp": fid(zh, (y + 1) % 4, c)}
-    down_dev = {"fsdp": fid(zh, (y + 3) % 4, c)}
     z_dev = {"fsdp": fid(1 - zh, y, c)}
+    y_dev = lambda rel: {"fsdp": fid(zh, (y + rel) % 4, c)}
     number = Slots()
     sent = []
 
@@ -86,9 +85,16 @@
     def x_dev(r):
         return {"dp": (d + r) % 4}
 
+    g_own = c * 4 + y
+    c_load = pltpu.make_async_copy(
+        cot.at[:, :, pl.ds(pl.multiple_of(g_own * COLS, COLS), COLS)], c_raw, local.at[9]
+    )
+    c_load.start()
+    t_load = pltpu.make_async_copy(tok, t_own.at[d], local.at[8])
+    t_load.start()
     w_loads = {}
-    for rel in (2, 3, 1, 0):
-        for cc in (0, 1):
+    for cc in (0, 1):
+        for rel in (2, 3, 1, 0):
             g = (c if cc == 0 else 1 - c) * 4 + (y + rel) % 4
             copy = pltpu.make_async_copy(
                 wgt.at[:, pl.ds(pl.multiple_of(g * COLS, COLS), COLS)], w_own.at[g],
@@ -96,10 +102,10 @@
             )
             copy.start()
             w_loads[rel, cc] = copy
-    t_load = pltpu.make_async_copy(tok, t_own.at[d], local.at[8])
-    t_load.start()
-    c_load = pltpu.make_async_copy(cot.at[d], ct.at[d], local.at[9])
-    c_load.start()
+    r_load = pltpu.make_async_copy(row_mom, r_mom, local.at[10])
+    r_load.start()
+    m_load = pltpu.make_async_copy(col_mom, c_mom, local.at[11])
+    m_load.start()
 
     barrier = pltpu.get_barrier_semaphore()
 
@@ -112,6 +118,9 @@
         return carry
 
     lax.fori_loop(1, 16, greet, 0)
+    c_load.wait()
+    for b in range(4):
+        c_out[b] = c_raw[:, b, :]
     pl.semaphore_wait(barrier, 30)
 
     for r in (1, 3, 2):
@@ -125,7 +134,7 @@
             ("w", rel), core_dev,
         )
     for r in (1, 3, 2):
-        start(cot.at[(d + r) % 4], ct.at[d], ("ct", r), x_dev(r))
+        start(c_out.at[(d + r) % 4], ct.at[d], ("ct", r), x_dev(r))
 
     have_w = set()
 
@@ -150,41 +159,19 @@
     def stage_products(k):
         dk = (d + k) % 4
         wait(t_peer.at[dk], ("tpeer", k))
-        sd[k] = product(k, 2).astype(BF16)
-        start(sd.at[k], rd.at[k], ("rd", k), up_dev if k in UP else down_dev)
-        if k in UP:
-            sn[k, 0] = product(k, 3).astype(BF16)
-            start(sn.at[k, 0], rp.at[k], ("rp", k), down_dev)
-            hn[k] = product(k, 1)
-        else:
-            sn[k, 0] = product(k, 1).astype(BF16)
-            start(sn.at[k, 0], rm.at[k], ("rm", k), up_dev)
-            hn[k] = product(k, 3)
+        for rel in (2, 1, 3):
+            so[k, rel - 1] = product(k, rel).astype(BF16)
+            start(so.at[k, rel - 1], rr.at[k, rel - 1], ("rs", k, rel), y_dev(rel))
         ho[k] = product(k, 0)
 
-    def stage_diagonal(k):
-        wait(rd.at[k], ("rd", k))
-        sn[k, 1] = (hn[k] + rd[k].astype(F32)).astype(BF16)
-        if k in UP:
-            start(sn.at[k, 1], rm.at[k], ("rm", k), up_dev)
-        else:
-            start(sn.at[k, 1], rp.at[k], ("rp", k), down_dev)
-
-    mine = pl.ds(pl.multiple_of(zh * HALF, HALF), HALF)
-    other = pl.ds(pl.multiple_of((1 - zh) * HALF, HALF), HALF)
-
     def stage_sum(k):
-        wait(rm.at[k], ("rm", k))
-        wait(rp.at[k], ("rp", k))
-        ho[k] = ho[k] + rm[k].astype(F32) + rp[k].astype(F32)
-        zs[k] = ho[k, other].astype(BF16)
+        total = ho[k]
+        for rel in (1, 3, 2):
+            wait(rr.at[k, rel - 1], ("rs", k, rel))
+            total = total + rr[k, rel - 1].astype(F32)
+        ho[k] = total
+        zs[k] = total.astype(BF16)
         start(zs.at[k], zr.at[k], ("z", k), z_dev)
-
-    g_own = c * 4 + y
-
-    def rows_of(k, zz):
-        dk = (d + k) % 4
-        return pl.ds(pl.multiple_of(dk * CHUNK + zz * HALF, HALF), HALF)
 
     def chunk_of(k):
         dk = (d + k) % 4
@@ -192,104 +179,54 @@
 
     def stage_slope(k):
         dk = (d + k) % 4
-        wait(zr.at[k], ("z", k))
         if k == 0:
-            c_load.wait()
+            upstream = c_out[d]
         else:
             wait(ct.at[dk], ("ct", 4 - k))
-        hidden = ho[k, mine] + zr[k].astype(F32)
-        sl[g_own, rows_of(k, zh)] = (ct[dk].astype(F32) * gelu_slope(hidden)).astype(BF16)
-        block = sl.at[g_own, rows_of(k, zh)]
-        start(block, block, ("zs", k), z_dev)
-
-    def stage_spread(k):
-        wait(sl.at[g_own, rows_of(k, 1 - zh)], ("zs", k))
+            upstream = ct[dk]
+        wait(zr.at[k], ("z", k))
+        hidden = ho[k] + zr[k].astype(F32)
+        sl[g_own, chunk_of(k)] = (upstream.astype(F32) * gelu_slope(hidden)).astype(BF16)
         block = sl.at[g_own, chunk_of(k)]
-        start(block, block, ("am", k), up_dev)
-        start(block, block, ("ap", k), down_dev)
+        for rel in (2, 1, 3):
+            start(block, block, ("ag", rel, k), y_dev(rel))
         start(block, block, ("core", 0, k), core_dev)
 
-    def stage_down(k):
-        block = sl.at[c * 4 + (y + 3) % 4, chunk_of(k)]
-        wait(block, ("am", k))
-        if k in UP:
-            start(block, block, ("ad", k), up_dev)
-        start(block, block, ("core", 3, k), core_dev)
-
-    def stage_up(k):
-        block = sl.at[c * 4 + (y + 1) % 4, chunk_of(k)]
-        wait(block, ("ap", k))
-        if k not in UP:
-            start(block, block, ("ad", k), down_dev)
-        start(block, block, ("core", 1, k), core_dev)
-
-    def stage_far(k):
-        block = sl.at[c * 4 + (y + 2) % 4, chunk_of(k)]
-        wait(block, ("ad", k))
-        start(block, block, ("core", 2, k), core_dev)
-
-    first = []
-
-    def group(rel, cc):
-        g = (c if cc == 0 else 1 - c) * 4 + (y + rel) % 4
+    def stage_arrive(k):
+        for rel in (1, 3, 2):
+            block = sl.at[c * 4 + (y + 4 - rel) % 4, chunk_of(k)]
+            wait(block, ("ag", rel, k))
+            start(block, block, ("core", 4 - rel, k), core_dev)
+
+    def group_at(rel, cc):
+        return (c if cc == 0 else 1 - c) * 4 + (y + rel) % 4
+
+    def group(rel, cc, sums):
+        g = group_at(rel, cc)
         if cc == 1:
-            w_loads[rel, 1].wait()
             for k in ORDER:
                 wait(sl.at[g, chunk_of(k)], ("core", rel, k))
         value = jnp.dot(t_tr[...], sl[g], preferred_element_type=F32)
         grad[g] = value
-        copy = pltpu.make_async_copy(grad.at[g], grad_out.at[g], local.at[10 + rel * 2 + cc])
-        copy.start()
         squares = value * value + tiny_term
-        col_buf[f, g] = jnp.sum(squares, axis=0, keepdims=True)
+        sums[...] = jnp.sum(squares, axis=0, keepdims=True)
         lanes = squares[:, :128] + squares[:, 128:]
+        if (rel, cc) == (0, 0):
+            row_acc[...] = lanes
+        else:
+            row_acc[...] += lanes
+
+    def group_terms(rel, cc):
+        g = group_at(rel, cc)
+        if cc == 1:
+            w_loads[rel, 1].wait()
         part = lax.dot_general(
             sl[g], w_own[g], (((1,), (1,)), ((), ())), preferred_element_type=F32
         )
-        if first:
-            row_acc[...] += lanes
+        if (rel, cc) == (0, 0):
+            terms[...] = part
+        else:
             terms[...] += part
-        else:
-            row_acc[...] = lanes
-            terms[...] = part
-        first.append(copy)
-
-    stages = (stage_products, stage_diagonal, stage_sum, stage_slope, stage_spread)
-    stage_tokens(0)
-    for step in range(4 + len(stages) - 1):
-        if step == 0:
-            stage_products(ORDER[0])
-            stage_tokens(1)
-            stage_tokens(3)
-            continue
-        if step == 2:
-            stage_tokens(2)
-        for s, stage in enumerate(stages):
-            if 0 <= step - s < 4:
-                stage(ORDER[step - s])
-        if step == 3:
-            for k in ORDER:
-                dk = (d + k) % 4
-                t_tr[:, pl.ds(pl.multiple_of(dk * CHUNK, CHUNK), CHUNK)] = t_own[dk].T
-    for k in ORDER:
-        stage_down(k)
-        stage_up(k)
-        if k == 1:
-            group(0, 0)
-    group(0, 1)
-    group(3, 0)
-    stage_far(0)
-    stage_far(1)
-    group(1, 0)
-    stage_far(3)
-    stage_far(2)
-    group(3, 1)
-    group(1, 1)
-    group(2, 0)
-    group(2, 1)
-
-    me = d * 4 + m
-    row_buf[me] = jnp.sum(row_acc[...].T, axis=0, keepdims=True)
 
     def to_fsdp(buf, slot, base):
         def one(j, carry):
@@ -339,8 +276,47 @@
 
         lax.fori_loop(1, 16, one, 0)
 
+    stage_tokens(0)
+    stage_products(0)
+    stage_tokens(1)
+    stage_tokens(3)
+    stage_products(1)
+    stage_products(3)
+    stage_sum(0)
+    stage_tokens(2)
+    stage_products(2)
+    stage_sum(1)
+    for k in ORDER:
+        dk = (d + k) % 4
+        t_tr[:, pl.ds(pl.multiple_of(dk * CHUNK, CHUNK), CHUNK)] = t_own[dk].T
+    stage_slope(0)
+    stage_sum(3)
+    stage_sum(2)
+    stage_slope(1)
+    stage_slope(3)
+    stage_arrive(0)
+    stage_slope(2)
+    group(0, 0, col_a.at[f, 0])
+    group_terms(0, 0)
+    stage_arrive(1)
+    stage_arrive(3)
+    group(0, 1, col_a.at[f, 1])
+    stage_arrive(2)
+    for i in range(2, 6):
+        group(*FIRST[i], col_a.at[f, i])
+    to_fsdp(col_a, f, 16)
+    for i in range(2):
+        group(*LAST[i], col_b.at[f, i])
+    to_fsdp(col_b, f, 64)
+
+    me = d * 4 + m
+    row_buf[me] = jnp.sum(row_acc[...].T, axis=0, keepdims=True)
+
     to_plane(row_buf, me, 0)
-    to_fsdp(col_buf, f, 16)
+    for i in range(1, 6):
+        group_terms(*FIRST[i])
+    for i in range(2):
+        group_terms(*LAST[i])
 
     for r in (2, 1, 3):
         dr = (d + r) % 4
@@ -351,17 +327,30 @@
     total = row_buf[0]
     for j in range(1, 16):
         total = total + row_buf[j]
-    row_new = DECAY * row_mom[...] + (1.0 - DECAY) * total / HID
+    r_load.wait()
+    row_new = DECAY * r_mom[...] + (1.0 - DECAY) * total / HID
     row_out[...] = row_new
     rcol = jnp.broadcast_to(lax.rsqrt(row_new), (128, ROWS)).T
     rcol_out[...] = rcol
     row_acc[...] = rcol * rcol
-    from_fsdp(col_buf, 16)
-    total = col_buf[0]
-    for j in range(1, 16):
-        total = total + col_buf[j]
-    col_new = DECAY * col_mom[...] + (1.0 - DECAY) * total / D
-    col_out[...] = col_new
+    from_fsdp(col_a, 16)
+    m_load.wait()
+
+    def col_finish(own_core, yy):
+        g = own_core * 4 + yy
+        total = jnp.zeros((1, COLS), F32)
+        for s in range(16):
+            place = ((yy - s // 2) % 4, own_core ^ (s % 2))
+            if place in FIRST:
+                total = total + col_a[s, FIRST.index(place)]
+            else:
+                total = total + col_b[s, LAST.index(place)]
+        col_out[g] = DECAY * c_mom[g] + (1.0 - DECAY) * total / D
+
+    from_fsdp(col_b, 64)
+    for own_core in (0, 1):
+        for yy in range(4):
+            col_finish(own_core, yy)
 
     def weigh(b, carry):
         rows = pl.ds(pl.multiple_of(b * 64, 64), 64)
@@ -410,8 +399,6 @@
 
     for copy in sent:
         copy.wait_send()
-    for copy in first:
-        copy.wait()
     assert len(number.numbers) <= N_SEMS, len(number.numbers)
 
 
@@ -420,13 +407,14 @@
     mean = jnp.sum(scal[:, 128:], axis=1, keepdims=True) / D
     rms = jnp.sqrt(mean * total / (D * HID))
     factor = jnp.sqrt(mean) / jnp.maximum(1.0, rms / clip_level)
-    rows = grad.shape[1]
-    left = rcol[...] * factor
+    rows = upd_out.shape[0] // 16
+    here = pl.ds(pl.multiple_of(pl.program_id(0) * rows, rows), rows)
+    left = rcol[here] * factor
     for g in range(GROUPS):
         right = lax.rsqrt(col_new[g])
         for h in (0, 1):
             lanes = slice(h * 128, h * 128 + 128)
-            upd_out[pl.ds(2 * g + h, rows, stride=16), :] = grad[g, :, lanes] * left * right[:, lanes]
+            upd_out[pl.ds(2 * g + h, rows, stride=16), :] = grad[g, here, lanes] * left * right[:, lanes]
 
     @pl.when(pl.program_id(0) == 0)
     def _():
@@ -437,12 +425,8 @@
 
 
 def per_device(tokens_in, weight, cotangent, row_moment, col_moment):
-    f = lax.axis_index("fsdp")
-    c, y, zh = f % 2, (f // 2) % 4, f // 8
-    upstream = lax.dynamic_slice(cotangent, (zh * HALF, 0, (c * 4 + y) * COLS), (HALF, 4, COLS))
-    upstream = upstream.swapaxes(0, 1)
     vmem = pl.BlockSpec(memory_space=pltpu.VMEM)
-    hbm = pl.BlockSpec(memory_space=pl.ANY)
+    hbm = pl.BlockSpec(memory_space=pltpu.HBM)
     sds = jax.ShapeDtypeStruct
     grad, inp, row_new, rcol, col_new, scal = pl.pallas_call(
         main_kernel,
@@ -455,42 +439,42 @@
             sds((GROUPS, 1, COLS), F32),
             sds((1, 256), F32),
         ),
-        in_specs=[hbm, hbm, hbm, vmem, vmem],
-        out_specs=(hbm, vmem, vmem, vmem, vmem, vmem),
+        in_specs=[hbm] * 5,
+        out_specs=(vmem, vmem, vmem, vmem, vmem, vmem),
         scratch_shapes=[
             pltpu.VMEM((4, CHUNK, ROWS), BF16),
             pltpu.VMEM((4, CHUNK, ROWS), BF16),
             pltpu.VMEM((ROWS, 4 * CHUNK), BF16),
             pltpu.VMEM((GROUPS, ROWS, COLS), BF16),
             pltpu.VMEM((4, ROWS, COLS), BF16),
-            pltpu.VMEM((4, HALF, COLS), BF16),
+            pltpu.VMEM((CHUNK, 4, COLS), BF16),
             pltpu.VMEM((4, CHUNK, COLS), BF16),
             pltpu.VMEM((4, CHUNK, COLS), BF16),
-            pltpu.VMEM((4, 2, CHUNK, COLS), BF16),
+            pltpu.VMEM((4, 3, CHUNK, COLS), BF16),
+            pltpu.VMEM((4, 3, CHUNK, COLS), BF16),
+            pltpu.VMEM((4, CHUNK, COLS), F32),
             pltpu.VMEM((4, CHUNK, COLS), BF16),
             pltpu.VMEM((4, CHUNK, COLS), BF16),
-            pltpu.VMEM((4, CHUNK, COLS), F32),
-            pltpu.VMEM((4, CHUNK, COLS), F32),
-            pltpu.VMEM((4, HALF, COLS), BF16),
-            pltpu.VMEM((4, HALF, COLS), BF16),
             pltpu.VMEM((GROUPS, 4 * CHUNK, COLS), BF16),
-            pltpu.VMEM((GROUPS, ROWS, COLS), F32),
             pltpu.VMEM((4 * CHUNK, ROWS), F32),
             pltpu.VMEM((4, CHUNK, ROWS), BF16),
             pltpu.VMEM((4, CHUNK, ROWS), BF16),
             pltpu.VMEM((CHUNK, ROWS), F32),
             pltpu.VMEM((4, CHUNK, 128), BF16),
             pltpu.VMEM((4, CHUNK, 128), BF16),
+            pltpu.VMEM((1, ROWS), F32),
+            pltpu.VMEM((GROUPS, 1, COLS), F32),
             pltpu.VMEM((ROWS, 128), F32),
             pltpu.VMEM((16, 1, ROWS), F32),
-            pltpu.VMEM((16, GROUPS, 1, COLS), F32),
+            pltpu.VMEM((16, 6, 1, COLS), F32),
+            pltpu.VMEM((16, 2, 1, COLS), F32),
             pltpu.VMEM((16, 1, 256), F32),
             pltpu.VMEM((16, 1, 256), F32),
             pltpu.SemaphoreType.DMA((N_SEMS,)),
             pltpu.SemaphoreType.DMA((N_SEMS,)),
-            pltpu.SemaphoreType.DMA((18,)),
-            pltpu.SemaphoreType.DMA((64,)),
-            pltpu.SemaphoreType.DMA((64,)),
+            pltpu.SemaphoreType.DMA((12,)),
+            pltpu.SemaphoreType.DMA((80,)),
+            pltpu.SemaphoreType.DMA((80,)),
         ],
         compiler_params=pltpu.CompilerParams(
             collective_id=0, has_side_effects=True, vmem_limit_bytes=44 * 1024 * 1024
@@ -499,7 +483,7 @@
     )(
         tokens_in,
         weight.reshape(ROWS, GROUPS * COLS),
-        upstream,
+        cotangent,
         row_moment.reshape(1, ROWS),
         col_moment.reshape(GROUPS, 1, COLS),
     )
@@ -518,8 +502,8 @@
             sds((1, 1), F32),
         ),
         in_specs=[
-            pl.BlockSpec((GROUPS, rows, COLS), lambda i: (0, i, 0)),
-            pl.BlockSpec((rows, 128), lambda i: (i, 0)),
+            vmem,
+            vmem,
             whole(1, ROWS),
             whole(GROUPS, 1, COLS),
             whole(1, 256),

time: 88.6 us -> 79.3 us (0.90)
  Pallas kernels: 82.2 us -> 72.9 us
    pallas_call x1, Pallas kernels: 78 us -> 69 us  [per_device(): pl.pallas_call(main_kernel, name='main', out_shape=(sds((GROUPS, ROWS, CO...]
    unnamed x11 -> x10, local copies, waits for them, and re-layouts: 5.42 us -> 5.46 us
where the time goes in v3:
time: 79.3 us; the launch traced here: 79 us
  Pallas kernels  72.9 us (92%)
  local copies, waits for them, and re-layouts  5.46 us (7%)
    pallas_call x1, Pallas kernels, per_device(): pl.pallas_call(main_kernel, name='main', out_shape=(sds((GROUPS, ROWS, CO...  69 us
    unnamed x10, local copies, waits for them, and re-layouts  5.46 us
    pallas_call x1, Pallas kernels, per_device(): pl.pallas_call(last_kernel, name='last', grid=(steps,), out_shape=(sds((R...  3.93 us

profile of v3, /device:TPU:1, one launch (start us, length us, event | category | flops | bytes accessed | tf_op | source)
XLA Modules:
  0.0 79.0 jit_solution(15296768505671411971)
XLA Ops:
  0.6 0.0 copy-start
  0.6 1.6 %copy-done = bf16[512,1,2048]{2,0,1:T(8,128)(2,1)S(1)} copy-done((bf16[512,1,2048]{2,0,1:T(8,128)(2,1)S(1)}, bf16[512,1,2048]{2,0,1:T(8,128)(2,1)}, u32[]{:S(2)}) %copy-start) | copy-done | bytes 2097176
  2.2 0.0 copy-start.1
  2.2 1.6 %copy-done.1 = bf16[128,4,2048]{2,1,0:T(4,128)(2,1)S(1)} copy-done((bf16[128,4,2048]{2,1,0:T(4,128)(2,1)S(1)}, bf16[128,4,2048]{2,1,0:T(4,128)(2,1)}, u32[]{:S(2)}) %copy-start.1) | copy-done | bytes 2097176
  3.8 0.0 copy-start.2
  3.8 0.9 %copy-done.2 = bf16[128,512]{1,0:T(8,128)(2,1)S(1)} copy-done((bf16[128,512]{1,0:T(8,128)(2,1)S(1)}, bf16[128,512]{1,0:T(8,128)(2,1)}, u32[]{:S(2)}) %copy-start.2) | copy-done | bytes 131096
  4.7 0.0 copy-start.3
  4.7 0.7 copy-done.3
  5.4 0.0 copy-start.4
  5.4 0.7 copy-done.4
  6.1 69.0 %main.1 = (f32[8,512,256]{2,1,0:T(8,128)S(1)}, bf16[128,128]{1,0:T(8,128)(2,1)S(1)}, f32[1,512]{1,0:T(1,128)S(1)}, f32[512,128]{1,0:T(8,128)S(1)}, f32[8,1,256]{2,1,0:T(1,128)S(1)}, /*index=5*/f32[1,256]{1,0:T(1,128)S(1)}) custom-call(bf16[128,512]{1,0:T(8,128)(2,1)S(1)} %copy-done.2, bf16[512,2048]{1,0:T(8,128)(2,1)S(1)} %bitcast.7, ...), custom_call_target="tpu_custom_call" | custom-call | flops 3221225472 | bytes 8388608 | tf_op jit(solution)/shard_map/main/pallas_call | solution.py:431
  75.1 3.9 %last.1 = (f32[8192,128]{1,0:T(8,128)}, f32[1,512]{1,0:T(1,128)}, f32[8,1,256]{2,1,0:T(1,128)}, bf16[128,128]{1,0:T(8,128)(2,1)}, f32[1,1]{1,0:T(1,128)}) custom-call(f32[8,512,256]{2,1,0:T(8,128)S(1)} %get-tuple-element.16.grad, f32[512,128]{1,0:T(8,128)S(1)} %get-tuple-element.17.rcol, f32[1,512]{1,0:T(1,128)S(1)} %get-tuple-element.18.row_new, ...), custom_call_target="tpu_custom_call" | custom-call | tf_op jit(solution)/shard_map/last/pallas_call | solution.py:493
Async XLA Ops:
  0.6 1.6 %copy-start = (bf16[512,1,2048]{2,0,1:T(8,128)(2,1)S(1)}, bf16[512,1,2048]{2,0,1:T(8,128)(2,1)}, u32[]{:S(2)}) copy-start(bf16[512,1,2048]{2,0,1:T(8,128)(2,1)} %param.6) | copy-start | bytes 6291460
  2.2 1.6 %copy-start.1 = (bf16[128,4,2048]{2,1,0:T(4,128)(2,1)S(1)}, bf16[128,4,2048]{2,1,0:T(4,128)(2,1)}, u32[]{:S(2)}) copy-start(bf16[128,4,2048]{2,1,0:T(4,128)(2,1)} %cot.1) | copy-start | bytes 6291460
  3.8 0.9 %copy-start.2 = (bf16[128,512]{1,0:T(8,128)(2,1)S(1)}, bf16[128,512]{1,0:T(8,128)(2,1)}, u32[]{:S(2)}) copy-start(bf16[128,512]{1,0:T(8,128)(2,1)} %tok.1) | copy-start | bytes 393220
  4.7 0.7 copy-start.3
  5.4 0.7 copy-start.4

commit v4 on v3

--- a/solution.py
+++ b/solution.py
@@ -27,6 +27,8 @@
 ORDER = (0, 1, 3, 2)
 FIRST = ((0, 0), (0, 1), (3, 0), (1, 0), (3, 1), (1, 1))
 LAST = ((2, 0), (2, 1))
+FAR_FSDP = (8, 7, 9, 6, 10, 5, 11, 4, 12, 3, 13, 2, 14, 1, 15)
+FAR_PLANE = (10, 9, 11, 8, 6, 14, 5, 7, 13, 15, 2, 1, 3, 4, 12)
 
 
 def gelu_slope(values):
@@ -50,12 +52,12 @@
 
 def main_kernel(
     tok, wgt, cot, row_mom, col_mom,
-    grad, inp_out, row_out, rcol_out, col_out, scal_out,
+    shape_out, inp_out, row_out, col_out, scal_out,
     t_own, t_peer, t_tr, w_own, w_peer, c_raw, c_out, ct,
-    so, rr, ho, zs, zr, sl, terms,
+    so, rr, ho, zs, zr, sl, grad, shape, terms,
     i_out, i_in, i_sum, j_out, j_in, r_mom, c_mom,
     row_acc, row_buf, col_a, col_b, one_buf, two_buf,
-    send, recv, local, peer_send, peer_recv,
+    send, recv, local, peer_send, peer_recv, heard,
 ):
     d, f, m = lax.axis_index("dp"), lax.axis_index("fsdp"), lax.axis_index("mp")
     c, y, zh = f % 2, (f // 2) % 4, f // 8
@@ -84,6 +86,12 @@
 
     def x_dev(r):
         return {"dp": (d + r) % 4}
+
+    barrier = pltpu.get_barrier_semaphore()
+    near = [core_dev, z_dev] + [y_dev(r) for r in (1, 3, 2)]
+    near += [{"dp": (d + r) % 4} for r in (1, 3, 2)] + [{"mp": (m + r) % 4} for r in (1, 2, 3)]
+    for dev in near:
+        pl.semaphore_signal(barrier, inc=1, device_id=dev, device_id_type=MESH)
 
     g_own = c * 4 + y
     c_load = pltpu.make_async_copy(
@@ -107,21 +115,10 @@
     m_load = pltpu.make_async_copy(col_mom, c_mom, local.at[11])
     m_load.start()
 
-    barrier = pltpu.get_barrier_semaphore()
-
-    def greet(j, carry):
-        pl.semaphore_signal(barrier, inc=1, device_id={"fsdp": (f + j) % 16}, device_id_type=MESH)
-        pl.semaphore_signal(
-            barrier, inc=1, device_id={"dp": (d + j // 4) % 4, "mp": (m + j % 4) % 4},
-            device_id_type=MESH,
-        )
-        return carry
-
-    lax.fori_loop(1, 16, greet, 0)
     c_load.wait()
     for b in range(4):
         c_out[b] = c_raw[:, b, :]
-    pl.semaphore_wait(barrier, 30)
+    pl.semaphore_wait(barrier, len(near))
 
     for r in (1, 3, 2):
         start(tok, t_own.at[d], ("tok", r), x_dev(r))
@@ -133,8 +130,8 @@
             wgt.at[:, pl.ds(pl.multiple_of(g * COLS, COLS), COLS)], w_peer.at[yy],
             ("w", rel), core_dev,
         )
-    for r in (1, 3, 2):
-        start(c_out.at[(d + r) % 4], ct.at[d], ("ct", r), x_dev(r))
+    for r in (1, 2, 3):
+        pl.semaphore_signal(heard, inc=1, device_id={"mp": (m + r) % 4}, device_id_type=MESH)
 
     have_w = set()
 
@@ -228,53 +225,44 @@
         else:
             terms[...] += part
 
+    late = []
+
+    def peer_copy(buf, slot, base, j, dev):
+        return pltpu.make_async_remote_copy(
+            src_ref=buf.at[slot], dst_ref=buf.at[slot], send_sem=peer_send.at[base + j],
+            recv_sem=peer_recv.at[base + j], device_id=dev, device_id_type=MESH,
+        )
+
+    def fsdp_dev(j):
+        return {"fsdp": (f + j) % 16}
+
+    def plane_dev(j):
+        return {"dp": (d + j // 4) % 4, "mp": (m + j % 4) % 4}
+
     def to_fsdp(buf, slot, base):
-        def one(j, carry):
-            pltpu.make_async_remote_copy(
-                src_ref=buf.at[slot], dst_ref=buf.at[slot], send_sem=peer_send.at[base + j],
-                recv_sem=peer_recv.at[base + j], device_id={"fsdp": (f + j) % 16},
-                device_id_type=MESH,
-            ).start()
-            return carry
-
-        lax.fori_loop(1, 16, one, 0)
+        for j in FAR_FSDP:
+            copy = peer_copy(buf, slot, base, j, fsdp_dev(j))
+            copy.start()
+            late.append(copy)
 
     def from_fsdp(buf, base):
-        def one(j, carry):
-            came = (f + 16 - j) % 16
-            pltpu.make_async_remote_copy(
-                src_ref=buf.at[came], dst_ref=buf.at[came], send_sem=peer_send.at[base + j],
-                recv_sem=peer_recv.at[base + j], device_id={"fsdp": (f + j) % 16},
-                device_id_type=MESH,
-            ).wait()
-            return carry
-
-        lax.fori_loop(1, 16, one, 0)
+        for j in FAR_FSDP[::-1]:
+            peer_copy(buf, (f + 16 - j) % 16, base, j, fsdp_dev(j)).wait_recv()
 
     def to_plane(buf, slot, base):
-        def one(j, carry):
-            pltpu.make_async_remote_copy(
-                src_ref=buf.at[slot], dst_ref=buf.at[slot], send_sem=peer_send.at[base + j],
-                recv_sem=peer_recv.at[base + j],
-                device_id={"dp": (d + j // 4) % 4, "mp": (m + j % 4) % 4},
-                device_id_type=MESH,
-            ).start()
-            return carry
-
-        lax.fori_loop(1, 16, one, 0)
+        for j in FAR_PLANE:
+            copy = peer_copy(buf, slot, base, j, plane_dev(j))
+            copy.start()
+            late.append(copy)
 
     def from_plane(buf, base):
-        def one(j, carry):
+        for j in FAR_PLANE[::-1]:
             came = ((d + 4 - j // 4) % 4) * 4 + (m + 4 - j % 4) % 4
-            pltpu.make_async_remote_copy(
-                src_ref=buf.at[came], dst_ref=buf.at[came], send_sem=peer_send.at[base + j],
-                recv_sem=peer_recv.at[base + j],
-                device_id={"dp": (d + j // 4) % 4, "mp": (m + j % 4) % 4},
-                device_id_type=MESH,
-            ).wait()
-            return carry
-
-        lax.fori_loop(1, 16, one, 0)
+            peer_copy(buf, came, base, j, plane_dev(j)).wait_recv()
+
+    def transpose(k):
+        dk = (d + k) % 4
+        t_tr[:, pl.ds(pl.multiple_of(dk * CHUNK, CHUNK), CHUNK)] = t_own[dk].T
 
     stage_tokens(0)
     stage_products(0)
@@ -284,21 +272,22 @@
     stage_products(3)
     stage_sum(0)
     stage_tokens(2)
+    for r in (1, 3, 2):
+        start(c_out.at[(d + r) % 4], ct.at[d], ("ct", r), x_dev(r))
     stage_products(2)
     stage_sum(1)
     for k in ORDER:
-        dk = (d + k) % 4
-        t_tr[:, pl.ds(pl.multiple_of(dk * CHUNK, CHUNK), CHUNK)] = t_own[dk].T
+        transpose(k)
     stage_slope(0)
     stage_sum(3)
     stage_sum(2)
     stage_slope(1)
+    stage_arrive(0)
     stage_slope(3)
-    stage_arrive(0)
+    stage_arrive(1)
     stage_slope(2)
     group(0, 0, col_a.at[f, 0])
     group_terms(0, 0)
-    stage_arrive(1)
     stage_arrive(3)
     group(0, 1, col_a.at[f, 1])
     stage_arrive(2)
@@ -312,6 +301,7 @@
     me = d * 4 + m
     row_buf[me] = jnp.sum(row_acc[...].T, axis=0, keepdims=True)
 
+    pl.semaphore_wait(heard, 3)
     to_plane(row_buf, me, 0)
     for i in range(1, 6):
         group_terms(*FIRST[i])
@@ -331,8 +321,7 @@
     row_new = DECAY * r_mom[...] + (1.0 - DECAY) * total / HID
     row_out[...] = row_new
     rcol = jnp.broadcast_to(lax.rsqrt(row_new), (128, ROWS)).T
-    rcol_out[...] = rcol
-    row_acc[...] = rcol * rcol
+    row_acc[...] = rcol
     from_fsdp(col_a, 16)
     m_load.wait()
 
@@ -360,13 +349,30 @@
             piece = grad[g, rows]
             piece = piece * piece * inverse
             acc = acc + piece[:, :128] + piece[:, 128:]
-        return carry + jnp.sum(acc * row_acc[rows], axis=0, keepdims=True)
+        right = row_acc[rows]
+        return carry + jnp.sum(acc * (right * right), axis=0, keepdims=True)
 
     u_lanes = lax.fori_loop(0, 8, weigh, jnp.zeros((1, 128), F32))
     a_lanes = (row_new[:, :128] + row_new[:, 128:256]) + (row_new[:, 256:384] + row_new[:, 384:])
     one_buf[f, :, :128] = u_lanes
     one_buf[f, :, 128:] = a_lanes
     to_fsdp(one_buf, f, 32)
+
+    def spread_rows(b, carry):
+        rows = pl.ds(pl.multiple_of(b * 64, 64), 64)
+        left = row_acc[rows]
+        for g in range(GROUPS):
+            right = lax.rsqrt(col_out[g])
+            for h in (0, 1):
+                lanes = slice(h * 128, h * 128 + 128)
+                shape[pl.ds(b * 1024 + 2 * g + h, 64, stride=16), :] = (
+                    grad[g, rows, lanes] * left * right[:, lanes]
+                )
+        block = pl.ds(pl.multiple_of(b * 1024, 1024), 1024)
+        pltpu.make_async_copy(shape.at[block], shape_out.at[block], peer_send.at[80 + b]).start()
+        return carry
+
+    lax.fori_loop(0, 8, spread_rows, 0)
     from_fsdp(one_buf, 32)
     total = one_buf[0]
     for j in range(1, 16):
@@ -397,24 +403,23 @@
         acc = acc + j_in[r].astype(F32)
     inp_out[...] = acc.astype(BF16)
 
-    for copy in sent:
+    def written(b, carry):
+        block = pl.ds(pl.multiple_of(b * 1024, 1024), 1024)
+        pltpu.make_async_copy(shape.at[block], shape_out.at[block], peer_send.at[80 + b]).wait()
+        return carry
+
+    lax.fori_loop(0, 8, written, 0)
+    for copy in sent + late:
         copy.wait_send()
     assert len(number.numbers) <= N_SEMS, len(number.numbers)
 
 
-def last_kernel(grad, rcol, row_new, col_new, scal, inp, upd_out, row_out, col_out, inp_out, rms_out):
+def last_kernel(shape, row_new, col_new, scal, inp, upd_out, row_out, col_out, inp_out, rms_out):
     total = jnp.sum(scal[:, :128], axis=1, keepdims=True)
     mean = jnp.sum(scal[:, 128:], axis=1, keepdims=True) / D
     rms = jnp.sqrt(mean * total / (D * HID))
     factor = jnp.sqrt(mean) / jnp.maximum(1.0, rms / clip_level)
-    rows = upd_out.shape[0] // 16
-    here = pl.ds(pl.multiple_of(pl.program_id(0) * rows, rows), rows)
-    left = rcol[here] * factor
-    for g in range(GROUPS):
-        right = lax.rsqrt(col_new[g])
-        for h in (0, 1):
-            lanes = slice(h * 128, h * 128 + 128)
-            upd_out[pl.ds(2 * g + h, rows, stride=16), :] = grad[g, here, lanes] * left * right[:, lanes]
+    upd_out[...] = shape[...] * factor
 
     @pl.when(pl.program_id(0) == 0)
     def _():
@@ -428,19 +433,18 @@
     vmem = pl.BlockSpec(memory_space=pltpu.VMEM)
     hbm = pl.BlockSpec(memory_space=pltpu.HBM)
     sds = jax.ShapeDtypeStruct
-    grad, inp, row_new, rcol, col_new, scal = pl.pallas_call(
+    shape, inp, row_new, col_new, scal = pl.pallas_call(
         main_kernel,
         name="main",
         out_shape=(
-            sds((GROUPS, ROWS, COLS), F32),
+            sds((ROWS * 16, 128), F32),
             sds((CHUNK, 128), BF16),
             sds((1, ROWS), F32),
-            sds((ROWS, 128), F32),
             sds((GROUPS, 1, COLS), F32),
             sds((1, 256), F32),
         ),
         in_specs=[hbm] * 5,
-        out_specs=(vmem, vmem, vmem, vmem, vmem, vmem),
+        out_specs=(hbm, vmem, vmem, vmem, vmem),
         scratch_shapes=[
             pltpu.VMEM((4, CHUNK, ROWS), BF16),
             pltpu.VMEM((4, CHUNK, ROWS), BF16),
@@ -456,6 +460,8 @@
             pltpu.VMEM((4, CHUNK, COLS), BF16),
             pltpu.VMEM((4, CHUNK, COLS), BF16),
             pltpu.VMEM((GROUPS, 4 * CHUNK, COLS), BF16),
+            pltpu.VMEM((GROUPS, ROWS, COLS), F32),
+            pltpu.VMEM((ROWS * 16, 128), F32),
             pltpu.VMEM((4 * CHUNK, ROWS), F32),
             pltpu.VMEM((4, CHUNK, ROWS), BF16),
             pltpu.VMEM((4, CHUNK, ROWS), BF16),
@@ -473,11 +479,12 @@
             pltpu.SemaphoreType.DMA((N_SEMS,)),
             pltpu.SemaphoreType.DMA((N_SEMS,)),
             pltpu.SemaphoreType.DMA((12,)),
-            pltpu.SemaphoreType.DMA((80,)),
-            pltpu.SemaphoreType.DMA((80,)),
+            pltpu.SemaphoreType.DMA((88,)),
+            pltpu.SemaphoreType.DMA((88,)),
+            pltpu.SemaphoreType.REGULAR,
         ],
         compiler_params=pltpu.CompilerParams(
-            collective_id=0, has_side_effects=True, vmem_limit_bytes=44 * 1024 * 1024
+            collective_id=0, has_side_effects=True, vmem_limit_bytes=60 * 1024 * 1024
         ),
         cost_estimate=pl.CostEstimate(flops=3 * 2**30, bytes_accessed=8 * 2**20, transcendentals=2**16),
     )(
@@ -487,7 +494,7 @@
         row_moment.reshape(1, ROWS),
         col_moment.reshape(GROUPS, 1, COLS),
     )
-    steps = 4
+    steps = 2
     rows = ROWS // steps
     whole = lambda *shape: pl.BlockSpec(shape, lambda i: (0,) * len(shape))
     update, row_new, col_new, input_grad, rms = pl.pallas_call(
@@ -502,8 +509,7 @@
             sds((1, 1), F32),
         ),
         in_specs=[
-            vmem,
-            vmem,
+            pl.BlockSpec((rows * 16, 128), lambda i: (i, 0)),
             whole(1, ROWS),
             whole(GROUPS, 1, COLS),
             whole(1, 256),
@@ -516,8 +522,8 @@
             whole(CHUNK, 128),
             whole(1, 1),
         ),
-        compiler_params=pltpu.CompilerParams(vmem_limit_bytes=44 * 1024 * 1024),
-    )(grad, rcol, row_new, col_new, scal, inp)
+        compiler_params=pltpu.CompilerParams(vmem_limit_bytes=60 * 1024 * 1024),
+    )(shape, row_new, col_new, scal, inp)
     return (
         input_grad,
         row_new.reshape(ROWS),

time: 79.3 us -> 70.5 us (0.89)
  local copies, waits for them, and re-layouts: 5.46 us -> 0 us
  Pallas kernels: 72.9 us -> 69.7 us
    unnamed x10 -> x0, local copies, waits for them, and re-layouts: 5.46 us -> none
    pallas_call x1, Pallas kernels: 69 us -> 65.8 us  [per_device(): pl.pallas_call(main_kernel, name='main', out_shape=(sds((ROWS * 16, 128),...]
where the time goes in v4:
time: 70.5 us; the launch traced here: 70.3 us
  Pallas kernels  69.7 us (99%)
    pallas_call x1, Pallas kernels, per_device(): pl.pallas_call(main_kernel, name='main', out_shape=(sds((ROWS * 16, 128),...  65.8 us
    pallas_call x1, Pallas kernels, per_device(): pl.pallas_call(last_kernel, name='last', grid=(steps,), out_shape=(sds((R...  3.88 us

profile of v4, /device:TPU:1, one launch (start us, length us, event | category | flops | bytes accessed | tf_op | source)
XLA Modules:
  0.0 70.3 jit_solution(15592467102753344327)
XLA Ops:
  0.6 65.8 %main.1 = (f32[8192,128]{1,0:T(8,128)}, bf16[128,128]{1,0:T(8,128)(2,1)}, f32[1,512]{1,0:T(1,128)}, f32[8,1,256]{2,1,0:T(1,128)}, f32[1,256]{1,0:T(1,128)}) custom-call(bf16[128,512]{1,0:T(8,128)(2,1)} %tok.1, bf16[512,2048]{1,0:T(8,128)(2,1)} %bitcast.8, bf16[128,4,2048]{2,1,0:T(4,128)(2,1)} %cot.1, f32[1,512]{1,0:T(1,128)} %bitcast.11, f32[8,1,256]{2,1,0:T(1,128)} %bitcast.9), custom_call_target="tpu_custom_call" | custom-call | flops 3221225472 | bytes 8388608 | tf_op jit(solution)/shard_map/main/pallas_call | solution.py:436
  66.5 3.9 %last.1 = (f32[8192,128]{1,0:T(8,128)}, f32[1,512]{1,0:T(1,128)}, f32[8,1,256]{2,1,0:T(1,128)}, bf16[128,128]{1,0:T(8,128)(2,1)}, f32[1,1]{1,0:T(1,128)}) custom-call(f32[8192,128]{1,0:T(8,128)} %get-tuple-element.15.shape, f32[1,512]{1,0:T(1,128)} %get-tuple-element.16.row_new, f32[8,1,256]{2,1,0:T(1,128)} %get-tuple-element.17.col_new, ...), custom_call_target="tpu_custom_call" | custom-call | tf_op jit(solution)/shard_map/last/pallas_call | solution.py:500

commit v5 on v4

--- a/solution.py
+++ b/solution.py
@@ -25,9 +25,10 @@
 ROWS = 512
 GROUPS = 8
 ORDER = (0, 1, 3, 2)
-FIRST = ((0, 0), (0, 1), (3, 0), (1, 0), (3, 1), (1, 1))
-LAST = ((2, 0), (2, 1))
+FIRST = ((0, 0), (0, 1), (3, 0), (1, 0), (2, 0))
+LAST = ((3, 1), (1, 1), (2, 1))
 FAR_FSDP = (8, 7, 9, 6, 10, 5, 11, 4, 12, 3, 13, 2, 14, 1, 15)
+FAR_CROSS = (10, 9, 11, 6, 14, 5, 7, 13, 15, 2, 8, 1, 3, 4, 12)
 FAR_PLANE = (10, 9, 11, 8, 6, 14, 5, 7, 13, 15, 2, 1, 3, 4, 12)
 
 
@@ -54,7 +55,7 @@
     tok, wgt, cot, row_mom, col_mom,
     shape_out, inp_out, row_out, col_out, scal_out,
     t_own, t_peer, t_tr, w_own, w_peer, c_raw, c_out, ct,
-    so, rr, ho, zs, zr, sl, grad, shape, terms,
+    so, rr, ho, zs, zr, sl, grad, shape,
     i_out, i_in, i_sum, j_out, j_in, r_mom, c_mom,
     row_acc, row_buf, col_a, col_b, one_buf, two_buf,
     send, recv, local, peer_send, peer_recv, heard,
@@ -94,15 +95,12 @@
         pl.semaphore_signal(barrier, inc=1, device_id=dev, device_id_type=MESH)
 
     g_own = c * 4 + y
-    c_load = pltpu.make_async_copy(
-        cot.at[:, :, pl.ds(pl.multiple_of(g_own * COLS, COLS), COLS)], c_raw, local.at[9]
-    )
-    c_load.start()
     t_load = pltpu.make_async_copy(tok, t_own.at[d], local.at[8])
     t_load.start()
     w_loads = {}
-    for cc in (0, 1):
-        for rel in (2, 3, 1, 0):
+
+    def load_weight(cc):
+        for rel in (2, 1, 3, 0):
             g = (c if cc == 0 else 1 - c) * 4 + (y + rel) % 4
             copy = pltpu.make_async_copy(
                 wgt.at[:, pl.ds(pl.multiple_of(g * COLS, COLS), COLS)], w_own.at[g],
@@ -110,26 +108,29 @@
             )
             copy.start()
             w_loads[rel, cc] = copy
-    r_load = pltpu.make_async_copy(row_mom, r_mom, local.at[10])
-    r_load.start()
-    m_load = pltpu.make_async_copy(col_mom, c_mom, local.at[11])
-    m_load.start()
-
-    c_load.wait()
-    for b in range(4):
-        c_out[b] = c_raw[:, b, :]
+
+    load_weight(0)
     pl.semaphore_wait(barrier, len(near))
 
     for r in (1, 3, 2):
         start(tok, t_own.at[d], ("tok", r), x_dev(r))
     start(tok, t_peer.at[d], ("tpeer", 0), core_dev)
-    for rel in (2, 3, 1, 0):
+    for rel in (2, 1, 3, 0):
         yy = (y + rel) % 4
         g = (1 - c) * 4 + yy
         start(
             wgt.at[:, pl.ds(pl.multiple_of(g * COLS, COLS), COLS)], w_peer.at[yy],
             ("w", rel), core_dev,
         )
+    c_load = pltpu.make_async_copy(
+        cot.at[:, :, pl.ds(pl.multiple_of(g_own * COLS, COLS), COLS)], c_raw, local.at[9]
+    )
+    c_load.start()
+    load_weight(1)
+    r_load = pltpu.make_async_copy(row_mom, r_mom, local.at[10])
+    r_load.start()
+    m_load = pltpu.make_async_copy(col_mom, c_mom, local.at[11])
+    m_load.start()
     for r in (1, 2, 3):
         pl.semaphore_signal(heard, inc=1, device_id={"mp": (m + r) % 4}, device_id_type=MESH)
 
@@ -200,9 +201,6 @@
 
     def group(rel, cc, sums):
         g = group_at(rel, cc)
-        if cc == 1:
-            for k in ORDER:
-                wait(sl.at[g, chunk_of(k)], ("core", rel, k))
         value = jnp.dot(t_tr[...], sl[g], preferred_element_type=F32)
         grad[g] = value
         squares = value * value + tiny_term
@@ -213,17 +211,25 @@
         else:
             row_acc[...] += lanes
 
-    def group_terms(rel, cc):
-        g = group_at(rel, cc)
-        if cc == 1:
-            w_loads[rel, 1].wait()
-        part = lax.dot_general(
-            sl[g], w_own[g], (((1,), (1,)), ((), ())), preferred_element_type=F32
-        )
-        if (rel, cc) == (0, 0):
-            terms[...] = part
+    def stage_core(k, rels):
+        for rel in rels:
+            wait(sl.at[group_at(rel, 1), chunk_of(k)], ("core", rel, k))
+
+    def input_terms(k):
+        if k == 0:
+            for rel in range(4):
+                w_loads[rel, 1].wait()
+        part = None
+        for g in range(GROUPS):
+            more = lax.dot_general(
+                sl[g, chunk_of(k)], w_own[g], (((1,), (1,)), ((), ())), preferred_element_type=F32
+            )
+            part = more if part is None else part + more
+        if k == 0:
+            i_sum[...] = part
         else:
-            terms[...] += part
+            i_out[k] = part.astype(BF16)
+            start(i_out.at[k], i_in.at[k], ("ix", k), x_dev(k))
 
     late = []
 
@@ -255,6 +261,36 @@
             copy.start()
             late.append(copy)
 
+    z8 = (zh * 4 + m) * 2 + c
+
+    def cross_dev(j):
+        return {"dp": (d + j // 4) % 4, "fsdp": fid(zh, (y + j % 4) % 4, c)}
+
+    def to_cross(buf, slot, base):
+        for j in FAR_CROSS:
+            copy = peer_copy(buf, slot, base, j, cross_dev(j))
+            copy.start()
+            late.append(copy)
+
+    def from_cross(buf, base):
+        for j in FAR_CROSS[::-1]:
+            came = ((d + 4 - j // 4) % 4) * 4 + (y + 4 - j % 4) % 4
+            peer_copy(buf, came, base, j, cross_dev(j)).wait_recv()
+
+    def pole_dev(j):
+        k = (z8 + j) % 16
+        return {"fsdp": fid(k // 8, y, k % 2), "mp": (k // 2) % 4}
+
+    def to_pole(buf, slot, base):
+        for j in FAR_FSDP:
+            copy = peer_copy(buf, slot, base, j, pole_dev(j))
+            copy.start()
+            late.append(copy)
+
+    def from_pole(buf, base):
+        for j in FAR_FSDP[::-1]:
+            peer_copy(buf, (z8 + 16 - j) % 16, base, j, pole_dev(j)).wait_recv()
+
     def from_plane(buf, base):
         for j in FAR_PLANE[::-1]:
             came = ((d + 4 - j // 4) % 4) * 4 + (m + 4 - j % 4) % 4
@@ -266,6 +302,9 @@
 
     stage_tokens(0)
     stage_products(0)
+    c_load.wait()
+    for b in range(4):
+        c_out[b] = c_raw[:, b, :]
     stage_tokens(1)
     stage_tokens(3)
     stage_products(1)
@@ -286,15 +325,21 @@
     stage_slope(3)
     stage_arrive(1)
     stage_slope(2)
+    stage_core(0, (0, 1, 3, 2))
+    input_terms(0)
     group(0, 0, col_a.at[f, 0])
-    group_terms(0, 0)
     stage_arrive(3)
+    stage_core(1, (0,))
+    stage_core(3, (0,))
+    stage_core(2, (0,))
     group(0, 1, col_a.at[f, 1])
     stage_arrive(2)
-    for i in range(2, 6):
+    for i in range(2, 5):
         group(*FIRST[i], col_a.at[f, i])
     to_fsdp(col_a, f, 16)
-    for i in range(2):
+    for k in (1, 3, 2):
+        stage_core(k, (1, 3, 2))
+    for i in range(3):
         group(*LAST[i], col_b.at[f, i])
     to_fsdp(col_b, f, 64)
 
@@ -303,16 +348,8 @@
 
     pl.semaphore_wait(heard, 3)
     to_plane(row_buf, me, 0)
-    for i in range(1, 6):
-        group_terms(*FIRST[i])
-    for i in range(2):
-        group_terms(*LAST[i])
-
-    for r in (2, 1, 3):
-        dr = (d + r) % 4
-        i_out[r] = terms[pl.ds(pl.multiple_of(dr * CHUNK, CHUNK), CHUNK)].astype(BF16)
-        start(i_out.at[r], i_in.at[r], ("ix", r), x_dev(r))
-
+    for k in (2, 1, 3):
+        input_terms(k)
     from_plane(row_buf, 0)
     total = row_buf[0]
     for j in range(1, 16):
@@ -354,9 +391,20 @@
 
     u_lanes = lax.fori_loop(0, 8, weigh, jnp.zeros((1, 128), F32))
     a_lanes = (row_new[:, :128] + row_new[:, 128:256]) + (row_new[:, 256:384] + row_new[:, 384:])
-    one_buf[f, :, :128] = u_lanes
-    one_buf[f, :, 128:] = a_lanes
-    to_fsdp(one_buf, f, 32)
+    here = d * 4 + y
+    one_buf[z8, :, :128] = u_lanes
+    one_buf[z8, :, 128:] = a_lanes
+    to_pole(one_buf, z8, 32)
+
+    acc = i_sum[...]
+    for r in (1, 3, 2):
+        wait(i_in.at[r], ("ix", r))
+        acc = acc + i_in[r].astype(F32)
+    i_sum[...] = acc
+    for r in (1, 3, 2):
+        mr = (m + r) % 4
+        j_out[r] = i_sum[:, pl.ds(pl.multiple_of(mr * 128, 128), 128)].astype(BF16)
+        start(j_out.at[r], j_in.at[r], ("jz", r), {"mp": mr})
 
     def spread_rows(b, carry):
         rows = pl.ds(pl.multiple_of(b * 64, 64), 64)
@@ -373,29 +421,18 @@
         return carry
 
     lax.fori_loop(0, 8, spread_rows, 0)
-    from_fsdp(one_buf, 32)
+    from_pole(one_buf, 32)
     total = one_buf[0]
     for j in range(1, 16):
         total = total + one_buf[j]
-    two_buf[me] = total
-    to_plane(two_buf, me, 48)
-
-    acc = terms[pl.ds(pl.multiple_of(d * CHUNK, CHUNK), CHUNK)]
-    for r in (1, 3, 2):
-        wait(i_in.at[r], ("ix", r))
-        acc = acc + i_in[r].astype(F32)
-    i_sum[...] = acc
-    for r in (1, 3, 2):
-        mr = (m + r) % 4
-        j_out[r] = i_sum[:, pl.ds(pl.multiple_of(mr * 128, 128), 128)].astype(BF16)
-        start(j_out.at[r], j_in.at[r], ("jz", r), {"mp": mr})
-
-    from_plane(two_buf, 48)
+    two_buf[here] = total
+    to_cross(two_buf, here, 48)
+
+    from_cross(two_buf, 48)
     total = two_buf[0]
     for j in range(1, 16):
         total = total + two_buf[j]
-    scal_out[:, :128] = total[:, :128]
-    scal_out[:, 128:] = two_buf[me][:, 128:]
+    scal_out[...] = total
 
     acc = i_sum[:, pl.ds(pl.multiple_of(m * 128, 128), 128)]
     for r in (1, 3, 2):
@@ -416,7 +453,7 @@
 
 def last_kernel(shape, row_new, col_new, scal, inp, upd_out, row_out, col_out, inp_out, rms_out):
     total = jnp.sum(scal[:, :128], axis=1, keepdims=True)
-    mean = jnp.sum(scal[:, 128:], axis=1, keepdims=True) / D
+    mean = jnp.sum(scal[:, 128:], axis=1, keepdims=True) / (16.0 * D)
     rms = jnp.sqrt(mean * total / (D * HID))
     factor = jnp.sqrt(mean) / jnp.maximum(1.0, rms / clip_level)
     upd_out[...] = shape[...] * factor
@@ -462,7 +499,6 @@
             pltpu.VMEM((GROUPS, 4 * CHUNK, COLS), BF16),
             pltpu.VMEM((GROUPS, ROWS, COLS), F32),
             pltpu.VMEM((ROWS * 16, 128), F32),
-            pltpu.VMEM((4 * CHUNK, ROWS), F32),
             pltpu.VMEM((4, CHUNK, ROWS), BF16),
             pltpu.VMEM((4, CHUNK, ROWS), BF16),
             pltpu.VMEM((CHUNK, ROWS), F32),
@@ -472,8 +508,8 @@
             pltpu.VMEM((GROUPS, 1, COLS), F32),
             pltpu.VMEM((ROWS, 128), F32),
             pltpu.VMEM((16, 1, ROWS), F32),
-            pltpu.VMEM((16, 6, 1, COLS), F32),
-            pltpu.VMEM((16, 2, 1, COLS), F32),
+            pltpu.VMEM((16, 5, 1, COLS), F32),
+            pltpu.VMEM((16, 3, 1, COLS), F32),
             pltpu.VMEM((16, 1, 256), F32),
             pltpu.VMEM((16, 1, 256), F32),
             pltpu.SemaphoreType.DMA((N_SEMS,)),

time: 70.5 us -> 68.6 us (0.973)
  Pallas kernels: 69.7 us -> 67.9 us
    pallas_call x1, Pallas kernels: 65.8 us -> 64 us  [per_device(): pl.pallas_call(main_kernel, name='main', out_shape=(sds((ROWS * 16, 128),...]
where the time goes in v5:
time: 68.6 us; the launch traced here: 68.5 us
  Pallas kernels  67.9 us (99%)
    pallas_call x1, Pallas kernels, per_device(): pl.pallas_call(main_kernel, name='main', out_shape=(sds((ROWS * 16, 128),...  64 us
    pallas_call x1, Pallas kernels, per_device(): pl.pallas_call(last_kernel, name='last', grid=(steps,), out_shape=(sds((R...  3.88 us

profile of v5, /device:TPU:1, one launch (start us, length us, event | category | flops | bytes accessed | tf_op | source)
XLA Modules:
  0.0 68.5 jit_solution(8203031908883842671)
XLA Ops:
  0.6 64.0 %main.1 = (f32[8192,128]{1,0:T(8,128)}, bf16[128,128]{1,0:T(8,128)(2,1)}, f32[1,512]{1,0:T(1,128)}, f32[8,1,256]{2,1,0:T(1,128)}, f32[1,256]{1,0:T(1,128)}) custom-call(bf16[128,512]{1,0:T(8,128)(2,1)} %tok.1, bf16[512,2048]{1,0:T(8,128)(2,1)} %bitcast.8, bf16[128,4,2048]{2,1,0:T(4,128)(2,1)} %cot.1, f32[1,512]{1,0:T(1,128)} %bitcast.11, f32[8,1,256]{2,1,0:T(1,128)} %bitcast.9), custom_call_target="tpu_custom_call" | custom-call | flops 3221225472 | bytes 8388608 | tf_op jit(solution)/shard_map/main/pallas_call | solution.py:473
  64.6 3.9 %last.1 = (f32[8192,128]{1,0:T(8,128)}, f32[1,512]{1,0:T(1,128)}, f32[8,1,256]{2,1,0:T(1,128)}, bf16[128,128]{1,0:T(8,128)(2,1)}, f32[1,1]{1,0:T(1,128)}) custom-call(f32[8192,128]{1,0:T(8,128)} %get-tuple-element.15.shape, f32[1,512]{1,0:T(1,128)} %get-tuple-element.16.row_new, f32[8,1,256]{2,1,0:T(1,128)} %get-tuple-element.17.col_new, ...), custom_call_target="tpu_custom_call" | custom-call | tf_op jit(solution)/shard_map/last/pallas_call | solution.py:536

commit v6 on v5

--- a/solution.py
+++ b/solution.py
@@ -186,9 +186,9 @@
         hidden = ho[k] + zr[k].astype(F32)
         sl[g_own, chunk_of(k)] = (upstream.astype(F32) * gelu_slope(hidden)).astype(BF16)
         block = sl.at[g_own, chunk_of(k)]
+        start(block, block, ("core", 0, k), core_dev)
         for rel in (2, 1, 3):
             start(block, block, ("ag", rel, k), y_dev(rel))
-        start(block, block, ("core", 0, k), core_dev)
 
     def stage_arrive(k):
         for rel in (1, 3, 2):
@@ -232,6 +232,11 @@
             start(i_out.at[k], i_in.at[k], ("ix", k), x_dev(k))
 
     late = []
+
+    def settle(copies):
+        for copy in copies:
+            copy.wait_send()
+        copies.clear()
 
     def peer_copy(buf, slot, base, j, dev):
         return pltpu.make_async_remote_copy(
@@ -343,6 +348,8 @@
         group(*LAST[i], col_b.at[f, i])
     to_fsdp(col_b, f, 64)
 
+    sent_before = list(sent)
+    sent.clear()
     me = d * 4 + m
     row_buf[me] = jnp.sum(row_acc[...].T, axis=0, keepdims=True)
 
@@ -350,6 +357,7 @@
     to_plane(row_buf, me, 0)
     for k in (2, 1, 3):
         input_terms(k)
+    settle(sent_before)
     from_plane(row_buf, 0)
     total = row_buf[0]
     for j in range(1, 16):
@@ -394,6 +402,8 @@
     here = d * 4 + y
     one_buf[z8, :, :128] = u_lanes
     one_buf[z8, :, 128:] = a_lanes
+    sums_before = list(late)
+    late.clear()
     to_pole(one_buf, z8, 32)
 
     acc = i_sum[...]
@@ -421,13 +431,24 @@
         return carry
 
     lax.fori_loop(0, 8, spread_rows, 0)
+    settle(sums_before)
     from_pole(one_buf, 32)
     total = one_buf[0]
     for j in range(1, 16):
         total = total + one_buf[j]
     two_buf[here] = total
+    pole_before = list(late)
+    late.clear()
     to_cross(two_buf, here, 48)
-
+    settle(pole_before)
+    settle(sent)
+
+    def written(b, carry):
+        block = pl.ds(pl.multiple_of(b * 1024, 1024), 1024)
+        pltpu.make_async_copy(shape.at[block], shape_out.at[block], peer_send.at[80 + b]).wait()
+        return carry
+
+    lax.fori_loop(0, 8, written, 0)
     from_cross(two_buf, 48)
     total = two_buf[0]
     for j in range(1, 16):
@@ -440,12 +461,6 @@
         acc = acc + j_in[r].astype(F32)
     inp_out[...] = acc.astype(BF16)
 
-    def written(b, carry):
-        block = pl.ds(pl.multiple_of(b * 1024, 1024), 1024)
-        pltpu.make_async_copy(shape.at[block], shape_out.at[block], peer_send.at[80 + b]).wait()
-        return carry
-
-    lax.fori_loop(0, 8, written, 0)
     for copy in sent + late:
         copy.wait_send()
     assert len(number.numbers) <= N_SEMS, len(number.numbers)

time: 68.6 us -> 68.2 us (level)
  no operation moved by 1% of the time
where the time goes in v6:
time: 68.2 us; the launch traced here: 68.1 us
  Pallas kernels  67.5 us (99%)
    pallas_call x1, Pallas kernels, per_device(): pl.pallas_call(main_kernel, name='main', out_shape=(sds((ROWS * 16, 128),...  63.6 us
    pallas_call x1, Pallas kernels, per_device(): pl.pallas_call(last_kernel, name='last', grid=(steps,), out_shape=(sds((R...  3.88 us

profile of v6, /device:TPU:1, one launch (start us, length us, event | category | flops | bytes accessed | tf_op | source)
XLA Modules:
  0.0 68.1 jit_solution(5396315178777556133)
XLA Ops:
  0.6 63.6 %main.1 = (f32[8192,128]{1,0:T(8,128)}, bf16[128,128]{1,0:T(8,128)(2,1)}, f32[1,512]{1,0:T(1,128)}, f32[8,1,256]{2,1,0:T(1,128)}, f32[1,256]{1,0:T(1,128)}) custom-call(bf16[128,512]{1,0:T(8,128)(2,1)} %tok.1, bf16[512,2048]{1,0:T(8,128)(2,1)} %bitcast.8, bf16[128,4,2048]{2,1,0:T(4,128)(2,1)} %cot.1, f32[1,512]{1,0:T(1,128)} %bitcast.11, f32[8,1,256]{2,1,0:T(1,128)} %bitcast.9), custom_call_target="tpu_custom_call" | custom-call | flops 3221225472 | bytes 8388608 | tf_op jit(solution)/shard_map/main/pallas_call | solution.py:488
  64.3 3.9 %last.1 = (f32[8192,128]{1,0:T(8,128)}, f32[1,512]{1,0:T(1,128)}, f32[8,1,256]{2,1,0:T(1,128)}, bf16[128,128]{1,0:T(8,128)(2,1)}, f32[1,1]{1,0:T(1,128)}) custom-call(f32[8192,128]{1,0:T(8,128)} %get-tuple-element.15.shape, f32[1,512]{1,0:T(1,128)} %get-tuple-element.16.row_new, f32[8,1,256]{2,1,0:T(1,128)} %get-tuple-element.17.col_new, ...), custom_call_target="tpu_custom_call" | custom-call | tf_op jit(solution)/shard_map/last/pallas_call | solution.py:551

commit v7 on v6

--- a/solution.py
+++ b/solution.py
@@ -328,8 +328,8 @@
     stage_slope(1)
     stage_arrive(0)
     stage_slope(3)
+    stage_slope(2)
     stage_arrive(1)
-    stage_slope(2)
     stage_core(0, (0, 1, 3, 2))
     input_terms(0)
     group(0, 0, col_a.at[f, 0])

time: 68.2 us -> 68.1 us (level)
  no operation moved by 1% of the time
where the time goes in v7:
time: 68.1 us; the launch traced here: 68 us
  Pallas kernels  67.4 us (99%)
    pallas_call x1, Pallas kernels, per_device(): pl.pallas_call(main_kernel, name='main', out_shape=(sds((ROWS * 16, 128),...  63.5 us
    pallas_call x1, Pallas kernels, per_device(): pl.pallas_call(last_kernel, name='last', grid=(steps,), out_shape=(sds((R...  3.88 us

profile of v7, /device:TPU:1, one launch (start us, length us, event | category | flops | bytes accessed | tf_op | source)
XLA Modules:
  0.0 68.0 jit_solution(2549270319363574657)
XLA Ops:
  0.6 63.5 %main.1 = (f32[8192,128]{1,0:T(8,128)}, bf16[128,128]{1,0:T(8,128)(2,1)}, f32[1,512]{1,0:T(1,128)}, f32[8,1,256]{2,1,0:T(1,128)}, f32[1,256]{1,0:T(1,128)}) custom-call(bf16[128,512]{1,0:T(8,128)(2,1)} %tok.1, bf16[512,2048]{1,0:T(8,128)(2,1)} %bitcast.8, bf16[128,4,2048]{2,1,0:T(4,128)(2,1)} %cot.1, f32[1,512]{1,0:T(1,128)} %bitcast.11, f32[8,1,256]{2,1,0:T(1,128)} %bitcast.9), custom_call_target="tpu_custom_call" | custom-call | flops 3221225472 | bytes 8388608 | tf_op jit(solution)/shard_map/main/pallas_call | solution.py:488
  64.1 3.9 %last.1 = (f32[8192,128]{1,0:T(8,128)}, f32[1,512]{1,0:T(1,128)}, f32[8,1,256]{2,1,0:T(1,128)}, bf16[128,128]{1,0:T(8,128)(2,1)}, f32[1,1]{1,0:T(1,128)}) custom-call(f32[8192,128]{1,0:T(8,128)} %get-tuple-element.15.shape, f32[1,512]{1,0:T(1,128)} %get-tuple-element.16.row_new, f32[8,1,256]{2,1,0:T(1,128)} %get-tuple-element.17.col_new, ...), custom_call_target="tpu_custom_call" | custom-call | tf_op jit(solution)/shard_map/last/pallas_call | solution.py:551
